TPU v7x, 32 devices: a whole 2x2x4 slice. The times are simulated.
32 devices in a mesh: ctx: 8 (over z, core), fsdp: 4 (over y, x).
Axes of the slice: x: 2, y: 2, z: 4, core: 2. Of those that a mesh axis runs over, the one named last changes fastest.
Arguments:
- hidden_in: bfloat16 [8, 2048, 2048], P('fsdp', 'ctx'), may hold values from -6 to 6
- cotangent: bfloat16 [8, 2048, 2048], P('fsdp', 'ctx'), may hold values from -6 to 6
- segment_ids: int32 [8, 2048], P('fsdp'), may hold values from 0 to 8, as said below
- w_query: bfloat16 [2048, 2048], P('fsdp'), may hold values from -0.25 to 0.25
- w_key: bfloat16 [2048, 1024], P('fsdp'), may hold values from -0.125 to 0.125
- w_value: bfloat16 [2048, 1024], P('fsdp'), may hold values from -0.125 to 0.125
- w_output: bfloat16 [2048, 2048], P('fsdp'), may hold values from -0.75 to 0.75
- w_gate: bfloat16 [2048, 8192], P('fsdp'), may hold values from -0.125 to 0.125
- w_up: bfloat16 [2048, 8192], P('fsdp'), may hold values from -0.125 to 0.125
- w_down: bfloat16 [8192, 2048], P('fsdp'), may hold values from -0.125 to 0.125
- attn_gain: bfloat16 [2048], P('fsdp'), may hold values from 0.5 to 1.5
- ffn_gain: bfloat16 [2048], P('fsdp'), may hold values from 0.5 to 1.5
Outputs:
- layer_out: bfloat16 [8, 2048, 2048], P('fsdp', 'ctx')
- grad_in: bfloat16 [8, 2048, 2048], P('fsdp', 'ctx')
- grad_query: float32 [2048, 2048], P('fsdp')
- grad_key: float32 [2048, 1024], P('fsdp')
- grad_value: float32 [2048, 1024], P('fsdp')
- grad_output: float32 [2048, 2048], P('fsdp')
- grad_gate: float32 [2048, 8192], P('fsdp')
- grad_up: float32 [2048, 8192], P('fsdp')
- grad_down: float32 [8192, 2048], P('fsdp')
- grad_attn_gain: float32 [2048], P('fsdp')
- grad_ffn_gain: float32 [2048], P('fsdp')
Inputs may be any that keep to these rules, and one draw needn't show every extreme that they name: `segment_ids`: in each group the first 1024 positions are 0; continuations 1 to 8 follow in order, each of 64 to 192 positions; in each group one has exactly 192 positions and one exactly 64.
All inputs are finite; a program needn't handle non-finite values.
Results may differ from a plain program's by a relative error of at most 0.02.
Values may be sent and summed in bfloat16 or wider, within the bound.
No kernel may reach another device: no remote copies, remote signals or barrier semaphores. Data moves between devices by JAX's collectives and lax.ppermute only.
A program may use at most 832 MiB of HBM per device.

v0:
```python
import math

import jax
import jax.numpy as jnp
from jax import lax
from jax.sharding import PartitionSpec as P

D = 2048
HEADS = 16
KVH = 8
HD = 128
FF = 8192
PROMPT = 1024
CONT = 8
QD = 2048
KVD = 1024


eps_norm = 1e-05
rope_base = 1000000.0
mask_fill = -1e30


def positions_of(segments):
    labels = jnp.arange(CONT + 1, dtype=jnp.int32)
    table = (segments[:, None] == labels[None, :]).astype(jnp.int32)
    counts = jnp.sum(table, axis=0)
    starts = jnp.cumsum(counts) - counts
    leading = jnp.sum(table * starts[None, :], axis=1)
    index = jnp.arange(segments.shape[0], dtype=jnp.int32)
    return index - leading + jnp.where(segments > 0, PROMPT, 0).astype(jnp.int32)


def rotary_tables(positions):
    half_width = HD // 2
    frequency = rope_base ** (-(jnp.arange(half_width, dtype=jnp.float32) * 2.0) / HD)
    angles = positions.astype(jnp.float32)[:, None] * frequency[None, :]
    return (jnp.cos(angles), jnp.sin(angles))


def rotate(values, cosine, sine, direction):
    rows_count = values.shape[0]
    heads_view = values.reshape(rows_count, -1, HD)
    former = heads_view[..., : HD // 2]
    latter = heads_view[..., HD // 2 :]
    cos_part = cosine[:, None, :]
    sin_part = sine[:, None, :] * direction
    turned = jnp.concatenate(
        [former * cos_part - latter * sin_part, latter * cos_part + former * sin_part], axis=-1
    )
    return turned.reshape(rows_count, -1)


def norm_parts(values, gain):
    inverse = lax.rsqrt(jnp.mean(values * values, axis=-1, keepdims=True) + eps_norm)
    scaled = values * inverse
    return (scaled * gain, scaled, inverse)


def norm_back(grad_out, values, scaled, inverse, gain):
    grad_scaled = grad_out * gain
    grad_gain = jnp.sum(grad_out * scaled, axis=0)
    along = jnp.mean(grad_scaled * values, axis=-1, keepdims=True)
    grad_values = inverse * grad_scaled - values * inverse * inverse * inverse * along
    return (grad_values, grad_gain)


def times_transpose(left, weight):
    return lax.dot_general(
        left, weight, (((1,), (1,)), ((), ())), preferred_element_type=jnp.float32
    )


def inner_rows(left, right):
    return lax.dot_general(
        left, right, (((0,), (0,)), ((), ())), preferred_element_type=jnp.float32
    )


def arrange(columns, outer_count, inner_count):
    rows_count, width = columns.shape
    piece_width = width // (outer_count * inner_count)
    return (
        columns.reshape(rows_count, outer_count, inner_count, piece_width)
        .transpose(0, 2, 1, 3)
        .reshape(rows_count, width)
    )


def local(
    hidden_in,
    cotangent,
    segment_ids,
    w_query,
    w_key,
    w_value,
    w_output,
    w_gate,
    w_up,
    w_down,
    attn_gain,
    ffn_gain,
):
    batches = hidden_in.shape[0]
    block_rows = hidden_in.shape[1]
    ctx_count = lax.axis_size("ctx")
    fsdp_count = lax.axis_size("fsdp")
    first_row = lax.axis_index("ctx") * block_rows
    scale = 1.0 / math.sqrt(HD)
    group_size = HEADS // KVH
    pieces = fsdp_count * ctx_count
    attn_width = QD + 2 * KVD
    ffn_blocks = 2 * FF // attn_width
    rows_up = D // pieces
    rows_out = QD // pieces
    rows_down = FF // pieces
    rows_both = rows_out + rows_down
    gain_first = jnp.zeros((D,), jnp.float32)
    gain_second = jnp.zeros((D,), jnp.float32)
    outputs = []
    grads_in = []
    kept_attn_in = []
    kept_ffn_in = []
    kept_right_attn = []
    kept_right_ffn = []
    kept_mixed = []
    kept_act = []
    kept_attn_grad = []
    kept_branch_grad = []
    (
        full_query,
        full_key,
        full_value,
        full_output,
        full_gate,
        full_up,
        full_down,
        full_attn_gain,
        full_ffn_gain,
    ) = (
        lax.all_gather(w_query, "fsdp", axis=0, tiled=True),
        lax.all_gather(w_key, "fsdp", axis=0, tiled=True),
        lax.all_gather(w_value, "fsdp", axis=0, tiled=True),
        lax.all_gather(w_output, "fsdp", axis=0, tiled=True),
        lax.all_gather(w_gate, "fsdp", axis=0, tiled=True),
        lax.all_gather(w_up, "fsdp", axis=0, tiled=True),
        lax.all_gather(w_down, "fsdp", axis=0, tiled=True),
        lax.all_gather(attn_gain, "fsdp", axis=0, tiled=True),
        lax.all_gather(ffn_gain, "fsdp", axis=0, tiled=True),
    )
    gain_attn = full_attn_gain.astype(jnp.float32)
    gain_ffn = full_ffn_gain.astype(jnp.float32)
    for micro_batch in range(batches):
        hidden = hidden_in[micro_batch].astype(jnp.float32)
        segments = segment_ids[micro_batch]
        query_segments = lax.dynamic_slice_in_dim(segments, first_row, block_rows)
        positions = lax.dynamic_slice_in_dim(positions_of(segments), first_row, block_rows)
        cosine, sine = rotary_tables(positions)
        normed_attn, scaled_attn, inverse_attn = norm_parts(hidden, gain_attn)
        attn_in = normed_attn.astype(jnp.bfloat16)
        queries = rotate(
            jnp.dot(attn_in, full_query, preferred_element_type=jnp.float32), cosine, sine, 1.0
        ).astype(jnp.bfloat16)
        keys_own = rotate(
            jnp.dot(attn_in, full_key, preferred_element_type=jnp.float32), cosine, sine, 1.0
        ).astype(jnp.bfloat16)
        values_own = jnp.dot(attn_in, full_value, preferred_element_type=jnp.float32).astype(
            jnp.bfloat16
        )
        keys_all, values_all = (
            lax.all_gather(keys_own, "ctx", axis=0, tiled=True),
            lax.all_gather(values_own, "ctx", axis=0, tiled=True),
        )
        tokens = keys_all.shape[0]
        query_view = queries.reshape(block_rows, KVH, group_size, HD)
        key_view = keys_all.reshape(tokens, KVH, HD)
        value_view = values_all.reshape(tokens, KVH, HD)
        scores = (
            jnp.einsum("qhgd,khd->hgqk", query_view, key_view, preferred_element_type=jnp.float32)
            * scale
        )
        query_index = first_row + jnp.arange(block_rows, dtype=jnp.int32)
        key_index = jnp.arange(tokens, dtype=jnp.int32)
        visible = (key_index[None, :] <= query_index[:, None]) & (
            (segments[None, :] == query_segments[:, None]) | (segments[None, :] == 0)
        )
        masked = jnp.where(visible[None, None], scores, mask_fill)
        highest_score = jnp.max(masked, axis=-1, keepdims=True)
        expos = jnp.exp(masked - highest_score)
        probs = expos / jnp.sum(expos, axis=-1, keepdims=True)
        probs_low = probs.astype(jnp.bfloat16)
        attended = jnp.einsum(
            "hgqk,khd->qhgd", probs_low, value_view, preferred_element_type=jnp.float32
        ).reshape(block_rows, QD)
        mixed = attended.astype(jnp.bfloat16)
        middle = hidden + jnp.dot(mixed, full_output, preferred_element_type=jnp.float32)
        normed_ffn, scaled_ffn, inverse_ffn = norm_parts(middle, gain_ffn)
        ffn_in = normed_ffn.astype(jnp.bfloat16)
        gate_pre = jnp.dot(ffn_in, full_gate, preferred_element_type=jnp.float32)
        up_pre = jnp.dot(ffn_in, full_up, preferred_element_type=jnp.float32)
        sigma = jax.nn.sigmoid(gate_pre)
        swish = gate_pre * sigma
        hidden_act = (swish * up_pre).astype(jnp.bfloat16)
        result = middle + jnp.dot(hidden_act, full_down, preferred_element_type=jnp.float32)
        outputs.append(result.astype(jnp.bfloat16))
        grad_top = cotangent[micro_batch].astype(jnp.float32)
        grad_branch = grad_top.astype(jnp.bfloat16)
        grad_act = times_transpose(grad_branch, full_down)
        grad_gate_pre = (grad_act * up_pre * sigma * (1.0 + gate_pre * (1.0 - sigma))).astype(
            jnp.bfloat16
        )
        grad_up_pre = (grad_act * swish).astype(jnp.bfloat16)
        grad_ffn_in = times_transpose(grad_gate_pre, full_gate) + times_transpose(
            grad_up_pre, full_up
        )
        grad_middle_part, gain_ffn_grad = norm_back(
            grad_ffn_in, middle, scaled_ffn, inverse_ffn, gain_ffn
        )
        grad_middle = grad_top + grad_middle_part
        grad_attn_out = grad_middle.astype(jnp.bfloat16)
        grad_mixed = times_transpose(grad_attn_out, full_output).astype(jnp.bfloat16)
        grad_view = grad_mixed.reshape(block_rows, KVH, group_size, HD)
        grad_probs = jnp.einsum(
            "qhgd,khd->hgqk", grad_view, value_view, preferred_element_type=jnp.float32
        )
        grad_scores = (
            probs * (grad_probs - jnp.sum(probs * grad_probs, axis=-1, keepdims=True))
        ).astype(jnp.bfloat16)
        grad_queries_raw = (
            jnp.einsum(
                "hgqk,khd->qhgd", grad_scores, key_view, preferred_element_type=jnp.float32
            ).reshape(block_rows, QD)
            * scale
        )
        grad_keys_part = (
            jnp.einsum(
                "hgqk,qhgd->khd", grad_scores, query_view, preferred_element_type=jnp.float32
            ).reshape(block_rows * lax.axis_size("ctx"), KVD)
            * scale
        )
        grad_values_part = jnp.einsum(
            "hgqk,qhgd->khd", probs_low, grad_view, preferred_element_type=jnp.float32
        ).reshape(block_rows * lax.axis_size("ctx"), KVD)
        key_grads = lax.psum_scatter(
            jnp.concatenate([grad_keys_part, grad_values_part], axis=1).astype(jnp.bfloat16),
            "ctx",
            scatter_dimension=0,
            tiled=True,
        ).astype(jnp.float32)
        grad_queries = rotate(grad_queries_raw, cosine, sine, -1.0).astype(jnp.bfloat16)
        grad_keys = rotate(key_grads[:, :KVD], cosine, sine, -1.0).astype(jnp.bfloat16)
        grad_values = key_grads[:, KVD:].astype(jnp.bfloat16)
        grad_attn_in = (
            times_transpose(grad_queries, full_query)
            + times_transpose(grad_keys, full_key)
            + times_transpose(grad_values, full_value)
        )
        grad_hidden_part, gain_attn_grad = norm_back(
            grad_attn_in, hidden, scaled_attn, inverse_attn, gain_attn
        )
        grads_in.append((grad_middle + grad_hidden_part).astype(jnp.bfloat16))
        gain_first = gain_first + gain_attn_grad
        gain_second = gain_second + gain_ffn_grad
        kept_attn_in.append(attn_in)
        kept_ffn_in.append(ffn_in)
        kept_right_attn.append(jnp.concatenate([grad_queries, grad_keys, grad_values], axis=1))
        kept_right_ffn.append(jnp.concatenate([grad_gate_pre, grad_up_pre], axis=1))
        kept_mixed.append(mixed)
        kept_act.append(hidden_act)
        kept_attn_grad.append(grad_attn_out)
        kept_branch_grad.append(grad_branch)
    left_attn = arrange(jnp.concatenate(kept_attn_in, axis=0), fsdp_count, ctx_count)
    left_ffn = arrange(jnp.concatenate(kept_ffn_in, axis=0), fsdp_count, ctx_count)
    right_attn = jnp.concatenate(kept_right_attn, axis=0)
    right_ffn = jnp.concatenate(kept_right_ffn, axis=0)
    all_rows = right_attn.shape[0]
    right_stack = jnp.concatenate(
        [right_attn[None], right_ffn.reshape(all_rows, ffn_blocks, attn_width).transpose(1, 0, 2)],
        axis=0,
    )
    left_mixed = arrange(jnp.concatenate(kept_mixed, axis=0), fsdp_count, ctx_count)
    left_act = arrange(jnp.concatenate(kept_act, axis=0), fsdp_count, ctx_count)
    attn_grads_all = jnp.concatenate(kept_attn_grad, axis=0)
    branch_grads_all = jnp.concatenate(kept_branch_grad, axis=0)
    left_stack = jnp.stack([left_attn] + [left_ffn] * ffn_blocks, axis=0)
    product = jnp.einsum(
        "btr,btc->rbc", left_stack, right_stack, preferred_element_type=jnp.float32
    )
    summed_up = lax.psum_scatter(
        product.reshape(lax.axis_size(("ctx", "fsdp")) * rows_up, (ffn_blocks + 1) * attn_width),
        ("ctx", "fsdp"),
        scatter_dimension=0,
        tiled=True,
    )
    block_count = lax.axis_size(("ctx", "fsdp")) * rows_both // rows_both
    term_out = inner_rows(left_mixed, attn_grads_all).reshape(block_count, rows_out, D)
    term_down = inner_rows(left_act, branch_grads_all).reshape(block_count, rows_down, D)
    summed_down = lax.psum_scatter(
        jnp.concatenate([term_out, term_down], axis=1).reshape(block_count * rows_both, D),
        ("ctx", "fsdp"),
        scatter_dimension=0,
        tiled=True,
    )
    summed_up, summed_down = (
        lax.all_gather(summed_up.astype(jnp.bfloat16), "ctx", axis=0, tiled=True).astype(
            summed_up.dtype
        ),
        lax.all_gather(summed_down.astype(jnp.bfloat16), "ctx", axis=0, tiled=True).astype(
            summed_down.dtype
        ),
    )
    gain_first, gain_second = lax.psum((gain_first, gain_second), ("ctx", "fsdp"))
    down_blocks = summed_down.reshape(-1, rows_both, D)
    grad_output = down_blocks[:, :rows_out].reshape(-1, D)
    grad_down = down_blocks[:, rows_out:].reshape(-1, D)
    grad_query = summed_up[:, :QD]
    grad_key = summed_up[:, QD : QD + KVD]
    grad_value = summed_up[:, QD + KVD : QD + 2 * KVD]
    grad_gate = summed_up[:, QD + 2 * KVD : QD + 2 * KVD + FF]
    grad_up = summed_up[:, QD + 2 * KVD + FF :]
    shard_rows = D // fsdp_count
    shard_start = lax.axis_index("fsdp") * shard_rows
    grad_attn_gain = lax.dynamic_slice_in_dim(gain_first, shard_start, shard_rows)
    grad_ffn_gain = lax.dynamic_slice_in_dim(gain_second, shard_start, shard_rows)
    return (
        jnp.stack(outputs),
        jnp.stack(grads_in),
        grad_query,
        grad_key,
        grad_value,
        grad_output,
        grad_gate,
        grad_up,
        grad_down,
        grad_attn_gain,
        grad_ffn_gain,
    )


def solution(mesh):
    placed = (
        P("fsdp", "ctx", None),
        P("fsdp", "ctx", None),
        P("fsdp", None),
        P("fsdp", None),
        P("fsdp", None),
        P("fsdp", None),
        P("fsdp", None),
        P("fsdp", None),
        P("fsdp", None),
        P("fsdp", None),
        P("fsdp"),
        P("fsdp"),
    )
    return jax.shard_map(
        local,
        mesh=mesh,
        in_specs=placed,
        out_specs=(
            P("fsdp", "ctx", None),
            P("fsdp", "ctx", None),
            P("fsdp", None),
            P("fsdp", None),
            P("fsdp", None),
            P("fsdp", None),
            P("fsdp", None),
            P("fsdp", None),
            P("fsdp", None),
            P("fsdp"),
            P("fsdp"),
        ),
        check_vma=False,
    )
```

profile of v0, /device:TPU:0, one launch (start us, length us, event | category | flops | bytes accessed | tf_op | source)
XLA Modules:
  0.0 7434.2 jit_solution(11147340021753289841)
XLA Ops:
  20.1 45.2 all-gather.16.cloned.1.call-done
  76.2 43.7 all-gather.20.cloned.1.call-done
  150.6 58.9 all-gather.24.cloned.1.call-done
  232.1 26.6 all-gather.34.cloned.1.call-done
  264.0 42.6 all-gather.18.cloned.1.call-done
  311.9 43.3 all-gather.22.cloned.1.call-done
  355.2 20.3 fusion.143
  389.8 53.1 all-gather.26.cloned.1.call-done
  450.0 42.9 all-gather.36.cloned.1.call-done
  492.9 24.4 fusion.142
  539.3 250.9 %all-gather.28.cloned.1.call-done = bf16[2048,8192]{1,0:T(8,128)(2,1)} async-done(((bf16[512,8192]{1,0:T(8,128)(2,1)}), bf16[2048,8192]{1,0:T(8,128)(2,1)}) %all-gather.28.cloned.1.call-update) | async-done | bytes 33554448 | tf_op jit(solution)/shard_map/all_gather | solution.py:145
  790.2 21.4 fusion.144
  811.6 277.5 %all-gather.30.cloned.1.call-done = bf16[2048,8192]{1,0:T(8,128)(2,1)} async-done(((bf16[512,8192]{1,0:T(8,128)(2,1)}), bf16[2048,8192]{1,0:T(8,128)(2,1)}) %all-gather.30.cloned.1.call-update) | async-done | bytes 33554448 | tf_op jit(solution)/shard_map/all_gather | solution.py:146
  1089.2 22.2 fusion.145
  1111.4 276.9 %all-gather.32.cloned.1.call-done = bf16[8192,2048]{1,0:T(8,128)(2,1)} async-done(((bf16[2048,2048]{1,0:T(8,128)(2,1)}), bf16[8192,2048]{1,0:T(8,128)(2,1)}) %all-gather.32.cloned.1.call-update) | async-done | bytes 33554448 | tf_op jit(solution)/shard_map/all_gather | solution.py:147
  1388.3 23.2 multiply_convert_fusion.2
  1481.4 23.0 multiply_convert_fusion
  1522.1 18.6 multiply_reduce_fusion
  1551.6 22.8 fusion.2
  1589.9 27.8 fusion.4
  1644.0 23.0 fusion.5
  1667.0 28.3 fusion.7
  1775.9 31.7 fusion.53
  1807.5 54.8 pad_maximum_fusion
  1908.0 22.6 copy.194
  1962.6 19.8 maximum_bitcast_fusion
  1982.4 71.6 fusion.10
  2054.0 151.2 %copy.156 = f32[2048,20480]{1,0:T(8,128)} copy(f32[2048,20480]{0,1:T(8,128)} %bitcast.91) | data formatting | bytes 335544320 | tf_op jit(solution)/shard_map/reshape | solution.py:290
  2205.3 1410.9 %reduce-scatter.11.cloned.1.call-done = f32[320,2048]{1,0:T(8,128)} async-done(((f32[10240,2048]{1,0:T(8,128)}), f32[320,2048]{1,0:T(8,128)}) %reduce-scatter.11.cloned.1.call-update) | async-done | bytes 2621456 | tf_op jit(solution)/shard_map/reduce_scatter | solution.py:298
  3619.3 3494.1 %reduce-scatter.9.cloned.1.call-done = f32[64,20480]{1,0:T(8,128)} async-done(((f32[2048,20480]{1,0:T(8,128)}), f32[64,20480]{1,0:T(8,128)}) %reduce-scatter.9.cloned.1.call-update) | async-done | bytes 5242896 | tf_op jit(solution)/shard_map/reduce_scatter | solution.py:289
  7172.2 45.7 all-reduce
  7242.2 160.2 %all-gather.38.cloned.1.call-done = bf16[512,20480]{1,0:T(8,128)(2,1)} async-done(((bf16[64,20480]{1,0:T(8,128)(2,1)}), bf16[512,20480]{1,0:T(8,128)(2,1)}) %all-gather.38.cloned.1.call-update) | async-done | bytes 20971536 | tf_op jit(solution)/shard_map/all_gather | solution.py:305
  (319 shorter events, 539.8 us)
Async XLA Ops:
  7.2 58.1 all-gather.16.cloned.1.call-start
  7.9 112.0 %all-gather.20.cloned.1.call-start = ((), (), s32[]{:S(2)}) async-start(), calls=%async_computation.6 | async-start | bytes 5242880 | tf_op jit(solution)/shard_map/all_gather | solution.py:142
  8.7 200.8 %all-gather.24.cloned.1.call-start = ((), (), s32[]{:S(2)}) async-start(), calls=%async_computation.8 | async-start | bytes 10485760 | tf_op jit(solution)/shard_map/all_gather | solution.py:141
  9.4 249.3 %all-gather.34.cloned.1.call-start = ((), (), s32[]{:S(2)}) async-start(), calls=%async_computation.13 | async-start | bytes 4718592 | tf_op jit(solution)/shard_map/all_gather | solution.py:172
  19.6 209.6 %copy-start.54 = (f32[4,1,512]{2,1,0:T(1,128)}, f32[4,1,512]{2,1,0:T(1,128)S(1)}, u32[]{:S(2)}) copy-start(f32[4,1,512]{2,1,0:T(1,128)S(1)} %convert_element_type.297) | copy-start | bytes 24580
  20.1 201.7 %copy-start.60 = (f32[256]{0:T(256)}, f32[256]{0:T(256)S(1)}, u32[]{:S(2)}) copy-start(f32[256]{0:T(256)S(1)} %add_rsqrt_fusion.1) | copy-start | bytes 3076
  69.6 237.0 %all-gather.18.cloned.1.call-start = ((), (), s32[]{:S(2)}) async-start(), calls=%async_computation.5 | async-start | bytes 4718592 | tf_op jit(solution)/shard_map/all_gather | solution.py:172
  69.7 159.5 %copy-start.63 = (f32[256]{0:T(256)}, f32[256]{0:T(256)S(1)}, u32[]{:S(2)}) copy-start(f32[256]{0:T(256)S(1)} %add_rsqrt_fusion.3) | copy-start | bytes 3076
  74.0 281.2 %all-gather.22.cloned.1.call-start = ((), (), s32[]{:S(2)}) async-start(), calls=%async_computation.7 | async-start | bytes 4718592 | tf_op jit(solution)/shard_map/all_gather | solution.py:171
  76.2 151.6 %copy-start.41 = (f32[256,64]{0,1:T(8,128)}, f32[256,64]{0,1:T(8,128)S(1)}, u32[]{:S(2)}) copy-start(f32[256,64]{0,1:T(8,128)S(1)} %get-tuple-element.83) | copy-start | bytes 196612
  76.2 155.4 %copy-start.39 = (f32[256,64]{0,1:T(8,128)}, f32[256,64]{0,1:T(8,128)S(1)}, u32[]{:S(2)}) copy-start(f32[256,64]{0,1:T(8,128)S(1)} %get-tuple-element.76) | copy-start | bytes 196612
  131.1 311.7 %all-gather.26.cloned.1.call-start = ((), (), s32[]{:S(2)}) async-start(), calls=%async_computation.9 | async-start | bytes 10485760 | tf_op jit(solution)/shard_map/all_gather | solution.py:144
  131.9 361.0 %all-gather.36.cloned.1.call-start = ((), (), s32[]{:S(2)}) async-start(), calls=%async_computation.14 | async-start | bytes 4718592 | tf_op jit(solution)/shard_map/all_gather | solution.py:171
  137.1 653.1 %all-gather.28.cloned.1.call-start = ((), (), s32[]{:S(2)}) async-start(), calls=%async_computation.10 | async-start | bytes 41943040 | tf_op jit(solution)/shard_map/all_gather | solution.py:145
  137.8 951.3 %all-gather.30.cloned.1.call-start = ((), (), s32[]{:S(2)}) async-start(), calls=%async_computation.11 | async-start | bytes 41943040 | tf_op jit(solution)/shard_map/all_gather | solution.py:146
  138.4 1249.8 %all-gather.32.cloned.1.call-start = ((), (), s32[]{:S(2)}) async-start(), calls=%async_computation.12 | async-start | bytes 41943040 | tf_op jit(solution)/shard_map/all_gather | solution.py:147
  139.2 1819.3 %reduce-scatter.7.cloned.1.call-start = ((), (), s32[]{:S(2)}) async-start(), calls=%async_computation.16 | async-start | bytes 9437184 | tf_op jit(solution)/shard_map/reduce_scatter | solution.py:244
  232.1 123.1 %copy-start.34 = (bf16[256,16,128]{0,2,1:T(8,128)(2,1)}, bf16[256,16,128]{0,2,1:T(8,128)(2,1)S(1)}, u32[]{:S(2)}) copy-start(bf16[256,16,128]{0,2,1:T(8,128)(2,1)S(1)} %pad_maximum_fusion.8) | copy-start | bytes 3145732
  389.8 60.2 copy-start.17
  539.3 549.8 %copy-start.26 = (bf16[256,2048]{1,0:T(8,128)(2,1)}, bf16[256,2048]{1,0:T(8,128)(2,1)S(1)}, u32[]{:S(2)}) copy-start(bf16[256,2048]{1,0:T(8,128)(2,1)S(1)} %multiply_convert_fusion.9) | copy-start | bytes 3145732
  811.6 576.6 %copy-start.12 = (bf16[2,256,2048]{2,1,0:T(8,128)(2,1)S(1)}, bf16[2,256,2048]{2,1,0:T(8,128)(2,1)}, u32[]{:S(2)}) copy-start(bf16[2,256,2048]{2,1,0:T(8,128)(2,1)} %param.13) | copy-start | bytes 6291460
  1504.4 42.3 slice-start
  1589.9 27.8 copy-start.36
  1636.5 324.1 %reduce-scatter.5.cloned.1.call-start = ((), (), s32[]{:S(2)}) async-start(), calls=%async_computation.15 | async-start | bytes 9437184 | tf_op jit(solution)/shard_map/reduce_scatter | solution.py:244
  1667.0 28.3 copy-start.35
  1730.1 1886.1 %reduce-scatter.11.cloned.1.call-start = ((), (), s32[]{:S(2)}) async-start(), calls=%async_computation.19 | async-start | bytes 86507520 | tf_op jit(solution)/shard_map/reduce_scatter | solution.py:298
  1862.3 5251.1 %reduce-scatter.9.cloned.1.call-start = ((), (), s32[]{:S(2)}) async-start(), calls=%async_computation.17 | async-start | bytes 173015040 | tf_op jit(solution)/shard_map/reduce_scatter | solution.py:289
  2205.2 5019.7 %all-gather.40.cloned.1.call-start = ((), (), s32[]{:S(2)}) async-start(), calls=%async_computation.20 | async-start | bytes 11796480 | tf_op jit(solution)/shard_map/all_gather | solution.py:308
  3619.2 3498.4 %copy-start.66 = (f32[2048]{0:T(1024)S(1)}, f32[2048]{0:T(1024)}, u32[]{:S(2)}) copy-start(f32[2048]{0:T(1024)} %get-tuple-element.13) | copy-start | bytes 24580
  3619.2 3498.4 %copy-start.67 = (f32[2048]{0:T(1024)S(1)}, f32[2048]{0:T(1024)}, u32[]{:S(2)}) copy-start(f32[2048]{0:T(1024)} %get-tuple-element.11) | copy-start | bytes 24580
  3619.2 3498.5 %copy-start.10 = (f32[256,2048]{1,0:T(8,128)S(1)}, f32[256,2048]{1,0:T(8,128)}, u32[]{:S(2)}) copy-start(f32[256,2048]{1,0:T(8,128)} %get-tuple-element.92) | copy-start | bytes 6291460
  3619.2 3783.2 %all-gather.38.cloned.1.call-start = ((), (), s32[]{:S(2)}) async-start(), calls=%async_computation.18 | async-start | bytes 23592960 | tf_op jit(solution)/shard_map/all_gather | solution.py:305
  (59 other events, 472.6 us)
Sparse Core Ops, SparseCore 0:
  9.9 55.3 all-gather.15
  67.2 52.7 all-gather.19
  121.8 87.6 all-gather.23
  211.5 47.1 all-gather.33
  260.7 45.8 all-gather.17
  308.6 46.5 all-gather.21
  357.0 85.8 all-gather.25
  445.1 47.7 all-gather.35
  494.7 295.4 all-gather.27
  791.9 297.2 all-gather.29
  1091.0 297.2 all-gather.31
  1636.7 89.6 reduce-scatter.6
  1730.2 89.7 reduce-scatter.4
  1862.5 1753.7 reduce-scatter.10
  3618.4 3494.9 reduce-scatter.8
  7115.6 100.7 all-gather.39
  7218.5 183.8 all-gather.37
where the time goes:
time: 7440 us; the launch traced here: 7430 us
  waiting for transfers between devices  6230 us (84%)
  matrix products  597 us (8%)
  local copies, waits for them, and re-layouts  314 us (4%)
  other arithmetic  212 us (3%)
    reduce_scatter x1, waiting for transfers between devices, local(): lax.psum_scatter(product.reshape(lax.axis_size(('ctx', 'fsdp')) * rows_up...  3490 us
    reduce_scatter x1, waiting for transfers between devices, local(): lax.psum_scatter(jnp.concatenate([term_out, term_down], axis=1).reshape(b...  1410 us
    all_gather x1, waiting for transfers between devices, local(): lax.all_gather(w_up, 'fsdp', axis=0, tiled=True)  278 us
    all_gather x1, waiting for transfers between devices, local(): lax.all_gather(w_down, 'fsdp', axis=0, tiled=True)  277 us
    all_gather x1, waiting for transfers between devices, local(): lax.all_gather(w_gate, 'fsdp', axis=0, tiled=True)  251 us
    all_gather x1, waiting for transfers between devices, local(): lax.all_gather(summed_up.astype(jnp.bfloat16), 'ctx', axis=0, tiled=True)  160 us
    reshape x1, local copies, waits for them, and re-layouts, local(): product.reshape(lax.axis_size(('ctx', 'fsdp')) * rows_up, (ffn_blocks + 1...  151 us
  transfers between devices with their start and end apart: 17, of which 14 were waited for; matrix products, arithmetic and copies ran while one was open for 11% of the time, Pallas kernels for 0%

commit v1 on v0

v1 whole, which is shorter than its diff:
```python
import functools
import math

import jax
import jax.numpy as jnp
from jax import lax
from jax.experimental import pallas as pl
from jax.experimental.pallas import tpu as pltpu
from jax.sharding import PartitionSpec as P

HD = 128
PROMPT = 1024
CONT = 8
LONGEST = 192

eps_norm = 1e-05
rope_base = 1000000.0
mask_fill = -1e30
log2_e = 1.4426950408889634
bf16 = jnp.bfloat16
f32 = jnp.float32
i32 = jnp.int32
MIB = 1024 * 1024
SMALL = pl.CostEstimate(flops=0, bytes_accessed=0, transcendentals=0)


def positions_of(segments, first_row, block):
    own = lax.dynamic_slice_in_dim(segments, first_row, block)
    leading = jnp.sum((segments[None, :] < own[:, None]).astype(i32), axis=1)
    index = first_row + jnp.arange(block, dtype=i32)
    return jnp.where(own > 0, index - leading + PROMPT, index)


def rotary_tables(positions):
    half_width = HD // 2
    frequency = rope_base ** (-(jnp.arange(half_width, dtype=f32) * 2.0) / HD)
    angles = positions.astype(f32)[:, None] * frequency[None, :]
    cosine, sine = jnp.cos(angles), jnp.sin(angles)
    return (
        jnp.concatenate([cosine, cosine], axis=1),
        jnp.concatenate([-sine, sine], axis=1),
    )


def norm_parts(values, gain):
    inverse = lax.rsqrt(jnp.mean(values * values, axis=-1, keepdims=True) + eps_norm)
    scaled = values * inverse
    return (scaled * gain, scaled, inverse)


def norm_back(grad_out, values, scaled, inverse, gain):
    grad_scaled = grad_out * gain
    grad_gain = jnp.sum(grad_out * scaled, axis=0)
    along = jnp.mean(grad_scaled * values, axis=-1, keepdims=True)
    grad_values = inverse * grad_scaled - values * inverse * inverse * inverse * along
    return (grad_values, grad_gain)


def dot(left, right, dims, out=f32):
    return lax.dot_general(left, right, (dims, ((), ())), preferred_element_type=out)


def nn(left, right, out=f32):
    return dot(left, right, ((1,), (0,)), out)


def nt(left, right, out=f32):
    return dot(left, right, ((1,), (1,)), out)


def tn(left, right, out=f32):
    return dot(left, right, ((0,), (0,)), out)


def product_kernel(left_ref, right_ref, o_ref):
    o_ref[...] = tn(left_ref[0], right_ref[0]).astype(bf16)


def product(left, right):
    left = left[None] if left.ndim == 2 else left
    right = right[None] if right.ndim == 2 else right
    lefts, depth, count = left.shape
    stack, _, cols = right.shape
    side = min(count, cols, 1024)
    across = cols // side
    return pl.pallas_call(
        product_kernel,
        out_shape=jax.ShapeDtypeStruct((count, stack * cols), bf16),
        grid=(stack, count // side, across),
        in_specs=[
            pl.BlockSpec((1, depth, side), lambda n, i, j: (n % lefts, 0, i)),
            pl.BlockSpec((1, depth, side), lambda n, i, j: (n, 0, j)),
        ],
        out_specs=pl.BlockSpec((side, side), lambda n, i, j: (i, n * across + j)),
        compiler_params=pltpu.CompilerParams(vmem_limit_bytes=48 * MIB),
        cost_estimate=SMALL,
    )(left, right)


def turned(u, cosine, sine):
    return u * cosine + pltpu.roll(u, HD // 2, 1) * sine


def project_kernel(x_ref, first_ref, last_ref, cos_ref, sin_ref, o_ref, *, second):
    acc = nn(x_ref[...], jnp.concatenate([first_ref[...], last_ref[...]], axis=1))
    cosine, sine = cos_ref[...], sin_ref[...]
    o_ref[:, :HD] = turned(acc[:, :HD], cosine, sine).astype(bf16)
    last = acc[:, HD:]
    if second:
        last = turned(last, cosine, sine)
    o_ref[:, HD:] = last.astype(bf16)


def project(x, weight, cosine, sine, second):
    count, depth = x.shape
    cols = weight.shape[1]
    steps = cols // (2 * HD)
    whole = lambda i: (0, 0)
    first = (lambda i: (0, 2 * i)) if second else (lambda i: (0, i))
    last = (lambda i: (0, 2 * i + 1)) if second else (lambda i: (0, i + steps))
    return pl.pallas_call(
        functools.partial(project_kernel, second=second),
        out_shape=jax.ShapeDtypeStruct((count, cols), bf16),
        grid=(steps,),
        in_specs=[
            pl.BlockSpec((count, depth), whole),
            pl.BlockSpec((depth, HD), first),
            pl.BlockSpec((depth, HD), last),
            pl.BlockSpec((count, HD), whole),
            pl.BlockSpec((count, HD), whole),
        ],
        out_specs=pl.BlockSpec((count, 2 * HD), lambda i: (0, i)),
        compiler_params=pltpu.CompilerParams(vmem_limit_bytes=32 * MIB),
        cost_estimate=SMALL,
    )(x, weight, weight, cosine, sine)


def unturn_kernel(x_ref, cos_ref, sin_ref, o_ref):
    keys = pl.program_id(0) < pl.num_programs(0) // 2

    @pl.when(keys)
    def _():
        o_ref[...] = turned(x_ref[...].astype(f32), cos_ref[...], -sin_ref[...]).astype(bf16)

    @pl.when(jnp.logical_not(keys))
    def _():
        o_ref[...] = x_ref[...]


def unturn(x, cosine, sine):
    count, cols = x.shape
    heads = cols // (2 * HD)
    whole = lambda i: (0, 0)
    return pl.pallas_call(
        unturn_kernel,
        out_shape=jax.ShapeDtypeStruct((count, cols), bf16),
        grid=(2 * heads,),
        in_specs=[
            pl.BlockSpec((count, HD), lambda i: (0, jnp.where(i < heads, 2 * i, 2 * (i - heads) + 1))),
            pl.BlockSpec((count, HD), whole),
            pl.BlockSpec((count, HD), whole),
        ],
        out_specs=pl.BlockSpec((count, HD), lambda i: (0, i)),
    )(x, cosine, sine)


def stacked(ref):
    return jnp.concatenate([ref[:, :HD], ref[:, HD:]], axis=0)


def scores_of(keys, bias, queries):
    s = nt(keys, queries) * (log2_e / math.sqrt(HD))
    return s + jnp.concatenate([bias, bias], axis=1)


def key_rows(places, n, block):
    return pl.ds(pl.multiple_of(places[n] * block, block), block)


def attend_kernel(flags, places, bias_ref, q_ref, kv_ref, o_ref, lse_ref, m_ref, l_ref, acc_ref):
    queries = stacked(q_ref)
    block = q_ref.shape[0]
    m_ref[...] = jnp.full_like(m_ref, mask_fill)
    l_ref[...] = jnp.zeros_like(l_ref)
    acc_ref[...] = jnp.zeros_like(acc_ref)
    for n in range(bias_ref.shape[0] // block):

        @pl.when(flags[n] > 0)
        def _():
            at = key_rows(places, n, block)
            s = scores_of(kv_ref[at, :HD], bias_ref[n * block : (n + 1) * block, :], queries)
            m_old = m_ref[...]
            m_new = jnp.maximum(m_old, jnp.max(s, axis=0, keepdims=True))
            p = jnp.exp2(s - m_new)
            alpha = jnp.exp2(m_old - m_new)
            l_ref[...] = l_ref[...] * alpha + jnp.sum(p, axis=0, keepdims=True)
            acc_ref[...] = acc_ref[...] * alpha + tn(kv_ref[at, HD:], p.astype(bf16))
            m_ref[...] = m_new

    total = l_ref[...]
    out = (acc_ref[...] / total).T.astype(bf16)
    o_ref[:, :HD] = out[:block]
    o_ref[:, HD:] = out[block:]
    lse_ref[0] = m_ref[...] + jnp.log(total) * log2_e


def attend(flags, places, bias, queries, kv, m, block):
    tokens, cols = kv.shape
    heads = cols // (2 * HD)
    keys = bias.shape[0]
    return pl.pallas_call(
        attend_kernel,
        out_shape=(
            jax.ShapeDtypeStruct((block, cols), bf16),
            jax.ShapeDtypeStruct((heads, 1, 2 * block), f32),
        ),
        grid=(heads,),
        in_specs=[
            pl.BlockSpec(memory_space=pltpu.SMEM),
            pl.BlockSpec(memory_space=pltpu.SMEM),
            pl.BlockSpec((keys, block), lambda h: (0, 0)),
            pl.BlockSpec((block, 2 * HD), lambda h: (m, h)),
            pl.BlockSpec((tokens, 2 * HD), lambda h: (0, h)),
        ],
        out_specs=(
            pl.BlockSpec((block, 2 * HD), lambda h: (0, h)),
            pl.BlockSpec((1, 1, 2 * block), lambda h: (h, 0, 0)),
        ),
        scratch_shapes=[
            pltpu.VMEM((1, 2 * block), f32),
            pltpu.VMEM((1, 2 * block), f32),
            pltpu.VMEM((HD, 2 * block), f32),
        ],
        compiler_params=pltpu.CompilerParams(vmem_limit_bytes=32 * MIB),
        cost_estimate=SMALL,
    )(flags, places, bias, queries, kv)


def attend_back_kernel(
    flags,
    places,
    bias_ref,
    q_ref,
    kv_ref,
    o_ref,
    go_ref,
    lse_ref,
    cos_ref,
    sin_ref,
    gq_ref,
    gshared_ref,
    gnear_ref,
    acc_ref,
):
    queries = stacked(q_ref)
    block = q_ref.shape[0]
    grads = stacked(go_ref)
    product = grads.astype(f32) * stacked(o_ref).astype(f32)
    delta = jnp.sum(product.T, axis=0, keepdims=True)
    lse = lse_ref[0]
    acc_ref[...] = jnp.zeros_like(acc_ref)
    scale = 1.0 / math.sqrt(HD)
    for n in range(bias_ref.shape[0] // block):
        shared = gshared_ref.shape[0] // block
        to_ref, k = (gshared_ref, n) if n < shared else (gnear_ref, n - shared)
        to = slice(k * block, (k + 1) * block)

        @pl.when(flags[n] > 0)
        def _():
            at = key_rows(places, n, block)
            p = jnp.exp2(scores_of(kv_ref[at, :HD], bias_ref[n * block : (n + 1) * block, :], queries) - lse)
            gp = nt(kv_ref[at, HD:], grads)
            gs = (p * (gp - delta)).astype(bf16)
            acc_ref[...] += tn(kv_ref[at, :HD], gs)
            to_ref[to, :HD] = (nn(gs, queries) * scale).astype(bf16)
            to_ref[to, HD:] = nn(p.astype(bf16), grads).astype(bf16)

        @pl.when(flags[n] == 0)
        def _():
            to_ref[to, :] = jnp.zeros((block, 2 * HD), bf16)

    out = acc_ref[...].T * scale
    cosine, sine = cos_ref[...], -sin_ref[...]
    gq_ref[:, :HD] = turned(out[:block], cosine, sine).astype(bf16)
    gq_ref[:, HD:] = turned(out[block:], cosine, sine).astype(bf16)


def attend_back(flags, places, bias, queries, kv, mixed, grad_mixed, lse, cosine, sine, m, block):
    tokens, cols = kv.shape
    heads = cols // (2 * HD)
    keys = bias.shape[0]
    near = (near_count(block) + 1) * block
    own = pl.BlockSpec((block, 2 * HD), lambda h: (0, h))
    far = pl.BlockSpec((keys - near, 2 * HD), lambda h: (0, h))
    close = pl.BlockSpec((near, 2 * HD), lambda h: (0, h))
    return pl.pallas_call(
        attend_back_kernel,
        out_shape=(
            jax.ShapeDtypeStruct((block, cols), bf16),
            jax.ShapeDtypeStruct((keys - near, cols), bf16),
            jax.ShapeDtypeStruct((near, cols), bf16),
        ),
        grid=(heads,),
        in_specs=[
            pl.BlockSpec(memory_space=pltpu.SMEM),
            pl.BlockSpec(memory_space=pltpu.SMEM),
            pl.BlockSpec((keys, block), lambda h: (0, 0)),
            pl.BlockSpec((block, 2 * HD), lambda h: (m, h)),
            pl.BlockSpec((tokens, 2 * HD), lambda h: (0, h)),
            own,
            own,
            pl.BlockSpec((1, 1, 2 * block), lambda h: (h, 0, 0)),
            pl.BlockSpec((block, HD), lambda h: (m, 0)),
            pl.BlockSpec((block, HD), lambda h: (m, 0)),
        ],
        out_specs=(own, far, close),
        scratch_shapes=[pltpu.VMEM((HD, 2 * block), f32)],
        compiler_params=pltpu.CompilerParams(vmem_limit_bytes=40 * MIB),
        cost_estimate=SMALL,
    )(flags, places, bias, queries, kv, mixed, grad_mixed, lse, cosine, sine)


FCOLS = 256
FROWS = 512


def ffn_kernel(b_ref, gz_ref, wg_ref, wu_ref, wd_ref, act_ref, grads_ref, y_ref, gb_ref, yacc, gacc):
    step = pl.program_id(0)
    last = pl.num_programs(0) - 1

    @pl.when(step == 0)
    def _():
        yacc[...] = jnp.zeros_like(yacc)
        gacc[...] = jnp.zeros_like(gacc)

    def body(i, carry):
        at = pl.ds(pl.multiple_of(i * FROWS, FROWS), FROWS)
        w = jnp.concatenate([wg_ref[...], wu_ref[...]], axis=1)
        both = nn(b_ref[at, :], w)
        gate, up = both[:, :FCOLS], both[:, FCOLS:]
        grad_act = nt(gz_ref[0, at, :], wd_ref[...])
        sigma = jax.nn.sigmoid(gate)
        swish = gate * sigma
        act = (swish * up).astype(bf16)
        grad_gate = (grad_act * up * sigma * (1.0 + gate * (1.0 - sigma))).astype(bf16)
        grad_up = (grad_act * swish).astype(bf16)
        act_ref[at, :] = act
        grads_ref[0, at, :] = grad_gate
        grads_ref[1, at, :] = grad_up
        yacc[at, :] += nn(act, wd_ref[...])
        gacc[at, :] += nt(jnp.concatenate([grad_gate, grad_up], axis=1), w)
        return carry

    lax.fori_loop(0, b_ref.shape[0] // FROWS, body, 0)

    @pl.when(step == last)
    def _():
        y_ref[...] = yacc[...].astype(bf16)
        gb_ref[...] = gacc[...].astype(bf16)


def feed_forward(b, gz, gate_up, down, m, batches, kept):
    count, width = b.shape
    cols = down.shape[0]
    steps = cols // FCOLS
    once = pl.Buffered(1)
    wide = jax.ShapeDtypeStruct((batches * count, cols), bf16)
    narrow = jax.ShapeDtypeStruct((count, width), bf16)
    tile = pl.BlockSpec((count, FCOLS), lambda j: (m, j))
    total = pl.BlockSpec((count, width), lambda j: (0, 0), pipeline_mode=once)

    def kernel(*refs):
        ffn_kernel(*refs[:5], *refs[5 + len(kept) :])

    return pl.pallas_call(
        kernel,
        out_shape=(wide, jax.ShapeDtypeStruct((2,) + wide.shape, bf16), narrow, narrow),
        grid=(steps,),
        in_specs=[
            pl.BlockSpec((count, width), lambda j: (0, 0), pipeline_mode=once),
            pl.BlockSpec((1, count, width), lambda j: (0, 0, 0), pipeline_mode=once),
            pl.BlockSpec((width, FCOLS), lambda j: (0, j)),
            pl.BlockSpec((width, FCOLS), lambda j: (0, j + steps)),
            pl.BlockSpec((FCOLS, width), lambda j: (j, 0)),
        ]
        + [pl.BlockSpec(memory_space=pl.ANY)] * len(kept),
        out_specs=(tile, pl.BlockSpec((2, count, FCOLS), lambda j: (0, m, j)), total, total),
        scratch_shapes=[pltpu.VMEM((count, width), f32), pltpu.VMEM((count, width), f32)],
        input_output_aliases={5 + i: i for i in range(len(kept))},
        compiler_params=pltpu.CompilerParams(vmem_limit_bytes=60 * MIB),
        cost_estimate=SMALL,
    )(b, gz, gate_up, gate_up, down, *kept)


def plane():
    return lax.axis_size("fsdp")


def bits_of(n):
    return [1 << i for i in range(n.bit_length() - 1)]


def fswap(bits):
    return lambda value: lax.ppermute(value, "fsdp", [(i, i ^ bits) for i in range(plane())])


def cswap(bits):
    return lambda value: lax.ppermute(value, "ctx", [(i, i ^ bits) for i in range(lax.axis_size("ctx"))])


def move(pairs):
    pairs = list(pairs)
    return lambda value: lax.ppermute(value, "ctx", pairs)


def rows(value, start, size):
    return lax.dynamic_slice_in_dim(value, start, size, axis=0)


def put_rows(target, value, start):
    return lax.dynamic_update_slice_in_dim(target, value, start, axis=0)


def plus(left, right):
    return left.astype(f32) + right.astype(f32)


def joined(parts):
    return jnp.concatenate(parts, axis=0) if len(parts) > 1 else parts[0]


def blank(rows_count, cols, kind, source):
    anywhere = pl.BlockSpec(memory_space=pl.ANY)
    return pl.pallas_call(
        lambda source_ref, out_ref: None,
        out_shape=jax.ShapeDtypeStruct((rows_count, cols), kind),
        in_specs=[anywhere],
        out_specs=anywhere,
    )(source)


def gate(values):
    if len(values) < 2:
        return list(values)
    anywhere = pl.BlockSpec(memory_space=pl.ANY)
    out = pl.pallas_call(
        lambda *refs: None,
        out_shape=[jax.ShapeDtypeStruct(v.shape, v.dtype) for v in values],
        in_specs=[anywhere] * len(values),
        out_specs=[anywhere] * len(values),
        input_output_aliases={i: i for i in range(len(values))},
        cost_estimate=SMALL,
    )(*values)
    return list(out)


class Flow:
    def __init__(self, steps, fresh=False):
        self.steps, self.result, self.want, self.got = steps, None, [], None
        self.fresh = fresh
        self.go(None)

    def go(self, given):
        try:
            self.want = self.steps.send(given)
        except StopIteration as stop:
            self.want, self.result = [], stop.value


class Line:
    def __init__(self):
        self.under_way = []

    def launch(self, *flows):
        flows = [f for f in flows if f.want]
        ready = gate([value for f in flows if f.fresh for value, _ in f.want])
        for f in flows:
            f.got = [fn(ready.pop(0) if f.fresh else value) for value, fn in f.want]
            self.under_way.append(f)

    def settle(self, *held):
        gated = gate([a for f in self.under_way for a in f.got] + list(held))
        for f in self.under_way:
            given, gated = gated[: len(f.got)], gated[len(f.got) :]
            f.go(given)
        self.under_way = []
        return gated[0] if len(held) == 1 else gated

    def finish(self, *flows):
        if self.under_way:
            self.settle()
        while any(f.want for f in flows):
            self.launch(*flows)
            self.settle()


def order():
    out = []
    for bits in (bits_of(plane()), bits_of(plane())[::-1]):
        ds = [0]
        for b in bits:
            ds = ds + [d ^ b for d in ds]
        out += ds
    return out


def gather_flow(own):
    half = own.shape[0] // 2
    first, last = own[:half], own[half:]
    bits = bits_of(plane())
    for a, b in zip(bits, bits[::-1]):
        got = yield [(first, fswap(a)), (last, fswap(b))]
        first = joined([first, got[0]])
        last = joined([last, got[1]])
    return joined([first, last])


def scatter_flow(parts):
    total = parts.shape[0] // 2
    first, last = parts[:total], parts[total:]
    bits = bits_of(plane())
    for a, b in zip(bits[::-1], bits):
        n = first.shape[0] // 2
        got = yield [(first[n:].astype(bf16), fswap(a)), (last[n:].astype(bf16), fswap(b))]
        first = plus(first[:n], got[0])
        last = plus(last[:n], got[1])
    return joined([first, last])


def weight_flow(own):
    shard, cols = own.shape
    me = lax.axis_index("fsdp")
    core = lax.axis_index("ctx") % 2
    half, part = shard // 2, shard // 4
    full = None
    mine = rows(own, core * half, half)
    first, last = mine[:part], mine[part:]
    bits = bits_of(plane())
    held, pending = [0], []
    for a, b in zip(bits + [None], bits[::-1] + [None]):
        want = [(value, cswap(1)) for value, _, _ in pending]
        if a is not None:
            want += [(first, fswap(a)), (last, fswap(b))]
        got = yield want
        if full is None:
            full = put_rows(blank(shard * plane(), cols, bf16, got[0]), own, me * shard)
        for n, (here, ds, offset) in enumerate(pending):
            for k, d in enumerate(ds):
                at = slice(k * part, (k + 1) * part)
                start = (me ^ d) * shard + offset
                full = put_rows(full, here[at], start + core * half)
                full = put_rows(full, got[n][at], start + (1 - core) * half)
        if a is not None:
            order_a = held_of(bits[: bits.index(a)])
            order_b = held_of(bits[::-1][: bits[::-1].index(b)])
            n = len(pending)
            pending = [
                (got[n], [d ^ a for d in order_a], 0),
                (got[n + 1], [d ^ b for d in order_b], part),
            ]
            first = joined([first, got[n]])
            last = joined([last, got[n + 1]])
    return full


def held_of(bits):
    ds = [0]
    for b in bits:
        ds = ds + [d ^ b for d in ds]
    return ds


def column_flow(weights, full, left):
    me = lax.axis_index("fsdp")
    core = lax.axis_index("ctx") % 2
    planes = plane()
    shard = weights.shape[0]
    half = shard // 2
    size = weights.shape[1] // planes

    def columns(j, start, count):
        return lax.dynamic_slice(weights, (start, (me ^ j) * size), (count, size))

    got = yield [(columns(j, core * half, half), fswap(j)) for j in range(1, planes)]
    full[0] = lax.dynamic_update_slice(full[0], columns(0, 0, shard), (me * shard, left))
    other = yield [(piece, cswap(1)) for piece in got]
    for j in range(1, planes):
        start = (me ^ j) * shard
        full[0] = lax.dynamic_update_slice(full[0], got[j - 1], (start + core * half, left))
        full[0] = lax.dynamic_update_slice(full[0], other[j - 1], (start + (1 - core) * half, left))
    return None


def shared_bits():
    bits = bits_of(lax.axis_size("ctx"))
    return bits[1:-1] + bits[:1]


def near_count(block):
    return -(-(LONGEST - 1) // block)


def slot_blocks(block):
    n = lax.axis_size("ctx")
    half = n // 2
    ctx = lax.axis_index("ctx")
    places = [((ctx % half) ^ d, True) for d in held_of(shared_bits())]
    count = near_count(block)
    return places + [(ctx - d, ctx - d >= half) for d in list(range(1, count + 1)) + [0]]


def keys_back_flow(shared, near):
    n = lax.axis_size("ctx")
    half = n // 2
    block = shared.shape[0] // half
    count = near_count(block)
    held = shared
    for b in reversed(shared_bits()):
        m = held.shape[0] // 2
        got = yield [(held[m:], cswap(b))]
        held = plus(held[:m], got[0]).astype(bf16)
    got = yield [(held, move((c + half, c) for c in range(half)))] + [
        (near[(d - 1) * block : d * block], move((c, c - d) for c in range(half + d, n))) for d in range(1, count + 1)
    ]
    prompt = plus(held, got[0])
    own = near[count * block :].astype(f32)
    for arrived in got[1:]:
        own = own + arrived.astype(f32)
    return jnp.where(lax.axis_index("ctx") < half, prompt, own).astype(bf16)


def core_flow(value, axis):
    size = value.shape[axis] // 2
    mine = (lax.axis_index("ctx") % 2) * size
    keep = lax.dynamic_slice_in_dim(value, mine, size, axis=axis)
    send = lax.dynamic_slice_in_dim(value, size - mine, size, axis=axis)
    got = yield [(send, cswap(1))]
    return plus(keep, got[0]).astype(bf16)


def rows_flow(partial):
    planes = plane()
    me = lax.axis_index("fsdp")
    shard, cols = partial.shape[0] // planes, partial.shape[1]
    p = yield from core_flow(partial.reshape(planes, shard, cols), 1)
    p = p.reshape(2 * planes, shard // 4, cols)
    p = joined([rows(p, (me ^ j) * 2 + n // planes, 1)[0] for n, j in enumerate(order())])
    s = yield from scatter_flow(p)
    return s.astype(bf16)


def cores_flow(half, widths):
    core = lax.axis_index("ctx") % 2
    count = half.shape[0]
    (other,) = yield [(half, cswap(1))]
    outs, left = [], 0
    for width in widths:
        out = blank(2 * count, width, f32, outs[-1] if outs else other)
        for source, start in ((half, core * count), (other, (1 - core) * count)):
            out = put_rows(out, source[:, left : left + width].astype(f32), start)
        outs.append(out)
        left += width
    return outs


def direct_flow(value, widths):
    chips = lax.axis_size("ctx") // 2
    place = lax.axis_index("ctx") // 2
    size = value.shape[0] // chips
    others = range(1, chips)
    got = yield [(rows(value, (place ^ d) * size, size), cswap(2 * d)) for d in others]
    own = rows(value, place * size, size).astype(f32)
    for arrived in got:
        own = own + arrived.astype(f32)
    own = own.astype(bf16)
    got = yield [(own, cswap(2 * d)) for d in others]
    half = put_rows(blank(value.shape[0], value.shape[1], bf16, got[0]), own, place * size)
    for d, arrived in zip(others, got):
        half = put_rows(half, arrived, (place ^ d) * size)
    return (yield from cores_flow(half, widths))


def exchange_flow(own, stack):
    planes, size, cols = own.shape
    me = lax.axis_index("fsdp")
    pieces = [lax.dynamic_index_in_dim(own, me ^ j, 0, keepdims=False) for j in range(planes)]
    got = yield [(pieces[j], fswap(j)) for j in range(1, planes)]
    line = blank(size, planes * cols, bf16, got[0])
    width = cols // stack
    for j, piece in enumerate(pieces[:1] + got):
        for n in range(stack):
            part = piece[:, n * width : (n + 1) * width]
            line = lax.dynamic_update_slice(line, part, (0, n * planes * width + (me ^ j) * width))
    return line


def total_flow(value):
    for fn in [cswap(b) for b in bits_of(lax.axis_size("ctx"))] + [fswap(b) for b in bits_of(plane())]:
        got = yield [(value, fn)]
        value = value + got[0]
    return value


def local(
    hidden_in,
    cotangent,
    segment_ids,
    w_query,
    w_key,
    w_value,
    w_output,
    w_gate,
    w_up,
    w_down,
    attn_gain,
    ffn_gain,
):
    batches, block, width = hidden_in.shape
    tokens = segment_ids.shape[1]
    ctx = lax.axis_index("ctx")
    planes = plane()
    me = lax.axis_index("fsdp")
    first_row = ctx * block
    qd = w_query.shape[1]
    kvd = w_key.shape[1]
    shard = w_query.shape[0]
    ff_own = w_down.shape[0]
    groups = range(batches)

    line = Line()
    keys_weight = Flow(weight_flow(jnp.concatenate([w_key, w_value], axis=1)))
    query_weight = Flow(weight_flow(w_query))
    out_weight = Flow(weight_flow(w_output))
    gate_up = [blank(width, 2 * ff_own, bf16, w_gate)]
    gate_weight = Flow(column_flow(w_gate, gate_up, 0))
    up_weight = Flow(column_flow(w_up, gate_up, ff_own))
    gz = [Flow(gather_flow(cotangent[m])) for m in groups]

    line.launch(keys_weight)
    gains_own = jnp.stack([attn_gain, ffn_gain])
    gains = jnp.zeros((2, width), bf16)
    for j in range(planes):
        piece = fswap(j)(gains_own) if j else gains_own
        gains = lax.dynamic_update_slice(gains, piece, (0, (me ^ j) * shard))
    gains = gains.astype(f32)
    gain_attn, gain_ffn = gains[0], gains[1]
    segment_ids = line.settle(segment_ids)
    segments_later = segment_ids

    line.launch(keys_weight)
    hidden = hidden_in.reshape(batches * block, width).astype(f32)
    normed_attn, scaled_attn, inverse_attn = norm_parts(hidden, gain_attn)
    attn_in = normed_attn.astype(bf16)
    tables = [rotary_tables(positions_of(segment_ids[m], first_row, block)) for m in groups]
    cosine = joined([t[0] for t in tables])
    sine = joined([t[1] for t in tables])
    line.settle()

    line.launch(keys_weight, query_weight)
    line.settle()
    line.finish(keys_weight)
    line.launch(query_weight, out_weight)
    kv_own = project(attn_in, keys_weight.result, cosine, sine, False)
    kv_own, segments_later = line.settle(kv_own, segments_later + 0)
    keys = [lax.all_gather(kv_own[m * block : (m + 1) * block], "ctx", axis=0, tiled=True) for m in groups]
    line.launch(query_weight, out_weight, *gz)
    line.settle()
    line.finish(query_weight)
    line.launch(out_weight, gate_weight)
    queries = project(attn_in, query_weight.result, cosine, sine, True)

    slots = slot_blocks(block)
    places = jnp.stack([jnp.where(counts, p, 0) for p, counts in slots])
    after_all = jnp.stack([jnp.where(counts, 0, tokens) for _, counts in slots])
    within = jnp.arange(block, dtype=i32)
    query_index = first_row + within
    key_index = (places[:, None] * block + after_all[:, None] + within[None, :]).reshape(-1)
    biases, flags = [], []
    for m in groups:
        segments = segments_later[m]
        query_segments = lax.dynamic_slice_in_dim(segments, first_row, block)
        chosen = (places[:, None] == jnp.arange(tokens // block, dtype=i32)[None, :]).astype(i32)
        key_segments = jnp.sum(chosen[:, :, None] * segments.reshape(1, -1, block), axis=1).reshape(-1)
        visible = (key_index[:, None] <= query_index[None, :]) & (
            (key_segments[:, None] == query_segments[None, :]) | (key_segments[:, None] == 0)
        )
        biases.append(jnp.where(visible, 0.0, mask_fill).astype(f32))
        flags.append(jnp.any(visible.reshape(-1, block * block), axis=1).astype(i32))

    mixed, lses, middles, normed, b_flows = [], [], [], [], []

    def attention(m):
        o, lse = line.settle(*attend(flags[m], places, biases[m], queries, keys[m], m, block))
        mixed.append(o)
        lses.append(lse)

    def to_feed_forward(m):
        middle = hidden[m * block : (m + 1) * block] + nn(mixed[m], out_weight.result)
        normed_ffn, scaled, inverse = norm_parts(middle, gain_ffn)
        middles.append(middle)
        normed.append((scaled, inverse))
        b_flows.append(Flow(gather_flow(normed_ffn.astype(bf16))))

    attention(0)
    line.finish(out_weight)
    line.launch(gate_weight, up_weight, *gz)
    to_feed_forward(0)
    for m in groups[1:]:
        attention(m)
        line.launch(*b_flows, up_weight)
        to_feed_forward(m)
    line.settle()
    line.launch(*b_flows)
    line.settle()

    wide, out_parts, grad_flows, b_all = (), [], [], []
    line.finish(gate_weight, up_weight)
    for m in groups:
        line.finish(b_flows[m], gz[m])
        line.launch(*b_flows, *grad_flows)
        b = b_flows[m].result
        b_all.append(b)
        *wide, out_part, grad_part = feed_forward(b, gz[m].result[None], gate_up[0], w_down, m, batches, tuple(wide))
        out_part, grad_part = line.settle(out_part, grad_part)
        out_parts.append(Flow(scatter_flow(out_part), True))
        grad_flows.append(Flow(scatter_flow(grad_part), True))
    act, grad_wide = wide

    line.launch(*grad_flows)
    down = line.settle(product(act, joined([f.result for f in gz])))
    down_part = lax.psum_scatter(down, "ctx", scatter_dimension=0, tiled=True)
    line.launch(*grad_flows)
    line.settle()
    line.finish(*grad_flows)

    grad_middles, gys, grads_mixed = [], [], []
    grad_ffn_gain = jnp.zeros((width,), f32)
    for m in groups:
        scaled, inverse = normed[m]
        grad_part, gain_part = norm_back(grad_flows[m].result, middles[m], scaled, inverse, gain_ffn)
        grad_ffn_gain = grad_ffn_gain + gain_part
        grad_middle = cotangent[m].astype(f32) + grad_part
        gy = grad_middle.astype(bf16)
        grads_mixed.append(nt(gy, out_weight.result).astype(bf16))
        grad_middles.append(grad_middle)
        gys.append(gy)
    key_backs, grads_q = [], []
    for m in groups:
        line.launch(*key_backs)
        gq, *gkv = attend_back(
            flags[m], places, biases[m], queries, keys[m], mixed[m], grads_mixed[m], lses[m], cosine, sine, m, block
        )
        if m == 0:
            gq, *gkv, grads_mixed[-1], down_part = line.settle(gq, *gkv, grads_mixed[-1], down_part)
        else:
            gq, *gkv = line.settle(gq, *gkv)
        grads_q.append(gq)
        key_backs.append(Flow(keys_back_flow(*gkv), True))
    down_all = lax.all_gather(down_part, "ctx", axis=0, tiled=True)

    gq = joined(grads_q)
    line.launch(*key_backs)
    grad_up, down_all = line.settle(product(joined(b_all), grad_wide), down_all)
    up_part = lax.psum_scatter(
        grad_up.reshape(planes, shard, 2 * ff_own), "ctx", scatter_dimension=1, tiled=True
    )
    line.launch(*key_backs)
    grad_attn = line.settle(product(jnp.stack([attn_in, joined(mixed)]), jnp.stack([gq, joined(gys)])))
    grad_attn = Flow(rows_flow(grad_attn), True)
    line.launch(*key_backs, grad_attn)
    line.settle()
    line.finish(*key_backs)
    line.launch(grad_attn)
    gkv = unturn(joined([f.result for f in key_backs]), cosine, sine)
    grad_keys, gkv = line.settle(product(attn_in, gkv), gkv)
    grad_keys = Flow(rows_flow(grad_keys), True)
    line.launch(grad_attn, grad_keys)
    grad_attn_in = nt(gq, query_weight.result) + nt(gkv, keys_weight.result)
    grad_part, grad_attn_gain = norm_back(grad_attn_in, hidden, scaled_attn, inverse_attn, gain_attn)
    grad_in = (joined(grad_middles) + grad_part).astype(bf16)
    gains_back = Flow(total_flow(line.settle(jnp.stack([grad_attn_gain, grad_ffn_gain]))))
    line.finish(grad_attn)
    attn_out = Flow(direct_flow(grad_attn.result, [qd, width]))
    line.launch(attn_out, grad_keys, gains_back)
    line.settle()
    line.launch(attn_out, grad_keys, gains_back)
    up_part = line.settle(up_part)
    line.finish(grad_keys)
    keys_out = Flow(direct_flow(grad_keys.result, [kvd, kvd]))
    up_line = Flow(exchange_flow(up_part, 2))
    line.launch(up_line, attn_out, keys_out, gains_back)
    line.settle()
    line.finish(up_line)
    up_all = lax.all_gather(up_line.result, "ctx", axis=0, tiled=True)
    line.launch(keys_out, gains_back, *out_parts)
    line.settle()
    line.launch(keys_out, gains_back, *out_parts)
    up_all = line.settle(up_all)
    line.finish(attn_out, keys_out, gains_back, *out_parts)
    gain_grads = lax.dynamic_slice(gains_back.result, (0, me * shard), (2, shard))
    outputs = [(middles[m] + out_parts[m].result).astype(bf16) for m in groups]
    return (
        jnp.stack(outputs),
        grad_in.reshape(batches, block, width),
        attn_out.result[0],
        keys_out.result[0],
        keys_out.result[1],
        attn_out.result[1],
        up_all[:, : planes * ff_own].astype(f32),
        up_all[:, planes * ff_own :].astype(f32),
        down_all.astype(f32),
        gain_grads[0],
        gain_grads[1],
    )


def solution(mesh):
    tokens3 = P("fsdp", "ctx", None)
    matrix = P("fsdp", None)
    return jax.shard_map(
        local,
        mesh=mesh,
        in_specs=(tokens3, tokens3) + (matrix,) * 8 + (P("fsdp"),) * 2,
        out_specs=(tokens3, tokens3) + (matrix,) * 7 + (P("fsdp"),) * 2,
        check_vma=False,
    )
```

time: 7440 us -> 1600 us (0.22)
  waiting for transfers between devices: 6230 us -> 581 us
  matrix products: 597 us -> 44.5 us
  Pallas kernels: 0 us -> 288 us
  starting transfers between devices: 0.68 us -> 149 us
    reduce_scatter x4 -> x2, waiting for transfers between devices: 4910 us -> 49 us  [the longest x1 49 us: local(): down_part = lax.psum_scatter(down, 'ctx', scatter_dimension=0, tiled=True)]
    all_gather x13 -> x4, waiting for transfers between devices: 1320 us -> 76.6 us  [the longest x1 52.2 us: local(): up_all = lax.all_gather(up_line.result, 'ctx', axis=0, tiled=True)]
    dot_general x41 -> x6, matrix products: 553 us -> 44.5 us  [dot(): lax.dot_general(left, right, (dims, ((), ())), preferred_element_type=out)]
    ppermute x0 -> x111, waiting for transfers between devices: none -> 455 us  [the longest x4 182 us: move(): return lambda value: lax.ppermute(value, 'ctx', pairs)]
    pallas_call x0 -> x61, Pallas kernels: none -> 288 us  [the longest x2 135 us: feed_forward(): pl.pallas_call(kernel, out_shape=(wide, jax.ShapeDtypeStruct((2,) + wide....]
    reshape x5 -> x0, local copies, waits for them, and re-layouts: 190 us -> none  [the longest x1 151 us: local(): product.reshape(lax.axis_size(('ctx', 'fsdp')) * rows_up, (ffn_blocks + 1...]
    ppermute x0 -> x111, starting transfers between devices: none -> 148 us  [the longest x66 73.9 us: fswap(): lax.ppermute(value, 'fsdp', [(i, i ^ bits) for i in range(plane())])]
    dynamic_update_slice x0 -> x71, local copies, waits for them, and re-layouts: none -> 126 us  [the longest x46 81.2 us: put_rows(): return lax.dynamic_update_slice_in_dim(target, value, start, axis=0)]
  transfers between devices with their start and end apart: 17 -> 117, of which waited for: 14 -> 41; matrix products, arithmetic and copies ran while one was open for 11% -> 25% of each run, Pallas kernels for 0% -> 18%
where the time goes in v1:
time: 1600 us; the launch traced here: 1590 us
  waiting for transfers between devices  581 us (36%)
  local copies, waits for them, and re-layouts  324 us (20%)
  Pallas kernels  288 us (18%)
  other arithmetic  185 us (12%)
  starting transfers between devices  149 us (9%)
  matrix products  44.5 us (3%)
  between operations  16.4 us (1%)
    ppermute x4, waiting for transfers between devices, move(): return lambda value: lax.ppermute(value, 'ctx', pairs)  182 us
    ppermute x66, waiting for transfers between devices, fswap(): lax.ppermute(value, 'fsdp', [(i, i ^ bits) for i in range(plane())])  157 us
    pallas_call x2, Pallas kernels, feed_forward(): pl.pallas_call(kernel, out_shape=(wide, jax.ShapeDtypeStruct((2,) + wide....  135 us
    unnamed x413, local copies, waits for them, and re-layouts  123 us
    ppermute x41, waiting for transfers between devices, cswap(): lax.ppermute(value, 'ctx', [(i, i ^ bits) for i in range(lax.axis_size('c...  115 us
    pallas_call x4, Pallas kernels, product(): pl.pallas_call(product_kernel, out_shape=jax.ShapeDtypeStruct((count, sta...  86.7 us
    dynamic_update_slice x46, local copies, waits for them, and re-layouts, put_rows(): return lax.dynamic_update_slice_in_dim(target, value, start, axis=0)  81.2 us
    ppermute x66, starting transfers between devices, fswap(): lax.ppermute(value, 'fsdp', [(i, i ^ bits) for i in range(plane())])  73.9 us
  transfers between devices with their start and end apart: 117, of which 41 were waited for; matrix products, arithmetic and copies ran while one was open for 25% of the time, Pallas kernels for 18%

profile of v1, /device:TPU:0, one launch (start us, length us, event | category | flops | bytes accessed | tf_op | source)
XLA Modules:
  0.0 1586.7 jit_solution(2795238385185838653)
XLA Ops:
  53.5 15.7 collective-permute-done.5.refs_3_
  172.6 13.8 collective-permute-done.23.refs_4_
  260.0 24.4 %all-gather.7.cloned.1.call-done.kv_ref = bf16[2048,2048]{1,0:T(8,128)(2,1)} async-done(((bf16[256,2048]{1,0:T(8,128)(2,1)}), bf16[2048,2048]{1,0:T(8,128)(2,1)}) %all-gather.7.cloned.1.call-update) | async-done | bytes 8388624 | tf_op jit(solution)/shard_map/all_gather | solution.py:765
  412.9 16.6 %collective-permute-done.50.refs_1_ = bf16[256,2048]{1,0:T(8,128)(2,1)} collective-permute-done((bf16[256,2048]{1,0:T(8,128)(2,1)S(1)}, bf16[256,2048]{1,0:T(8,128)(2,1)}, u32[]{:S(2)}, u32[]{:S(2)}) %collective-permute-start.50) | collective-permute-done | bytes 1048608 | tf_op jit(solution)/shard_map/ppermute | solution.py:404
  449.5 67.7 %shard_map.220 = (bf16[2048,2048]{1,0:T(8,128)(2,1)}, bf16[2,2048,2048]{2,1,0:T(8,128)(2,1)}, bf16[1024,2048]{1,0:T(8,128)(2,1)}, bf16[1024,2048]{1,0:T(8,128)(2,1)}) custom-call(bf16[1024,2048]{1,0:T(8,128)(2,1)} %get-tuple-element.478.refs_0_, bf16[1,1024,2048]{2,1,0:T(8,128)(2,1)} %bitcast.168, ...), custom_call_target="tpu_custom_call" | custom-call | tf_op jit(solution)/shard_map/pallas_call | solution.py:375
  538.7 67.6 %shard_map.223 = (bf16[2048,2048]{1,0:T(8,128)(2,1)}, bf16[2,2048,2048]{2,1,0:T(8,128)(2,1)}, bf16[1024,2048]{1,0:T(8,128)(2,1)}, bf16[1024,2048]{1,0:T(8,128)(2,1)}) custom-call(bf16[1024,2048]{1,0:T(8,128)(2,1)} %get-tuple-element.474.refs_0_, bf16[1,1024,2048]{2,1,0:T(8,128)(2,1)} %bitcast.167, ...), custom_call_target="tpu_custom_call", output_to_operand_aliasing={{0}: (5, {}), {1}: (6, {})} | custom-call | tf_op jit(solution)/shard_map/pallas_call | solution.py:375
  617.3 23.0 %shard_map.226.refs_4_ = bf16[2048,2048]{1,0:T(8,128)(2,1)} custom-call(bf16[1,2048,2048]{2,1,0:T(8,128)(2,1)} %bitcast.162, bf16[1,2048,2048]{2,1,0:T(8,128)(2,1)} %bitcast.166), custom_call_target="tpu_custom_call" | custom-call | tf_op jit(solution)/shard_map/pallas_call | solution.py:86
  683.3 11.4 shard_map.228
  705.9 49.0 %reduce-scatter.3.cloned.1.call-done.refs_4_ = bf16[256,2048]{1,0:T(8,128)(2,1)} async-done(((bf16[2048,2048]{1,0:T(8,128)(2,1)}), bf16[256,2048]{1,0:T(8,128)(2,1)}) %reduce-scatter.3.cloned.1.call-update) | async-done | bytes 1048592 | tf_op jit(solution)/shard_map/reduce_scatter | solution.py:831
  757.6 11.6 shard_map.232
  785.4 9.3 collective-permute-start.64
  794.7 41.3 %shard_map.235.refs_2_ = bf16[2048,4096]{1,0:T(8,128)(2,1)} custom-call(bf16[1,2048,2048]{2,1,0:T(8,128)(2,1)} %bitcast.29.left_ref, bf16[2,2048,2048]{2,1,0:T(8,128)(2,1)} %get-tuple-element.300.right_ref), custom_call_target="tpu_custom_call" | custom-call | tf_op jit(solution)/shard_map/pallas_call | solution.py:86
  836.0 19.6 %collective-permute-done.64.refs_0_ = bf16[256,2048]{1,0:T(8,128)(2,1)S(1)} collective-permute-done((bf16[256,2048]{1,0:T(8,128)(2,1)}, bf16[256,2048]{1,0:T(8,128)(2,1)S(1)}, u32[]{:S(2)}, u32[]{:S(2)}) %collective-permute-start.64) | collective-permute-done | bytes 1048608 | tf_op jit(solution)/shard_map/ppermute | solution.py:408
  884.2 15.5 shard_map.238.refs_3_
  899.6 54.1 %collective-permute-done.66.refs_0_ = bf16[256,2048]{1,0:T(8,128)(2,1)} collective-permute-done((bf16[256,2048]{1,0:T(8,128)(2,1)}, bf16[256,2048]{1,0:T(8,128)(2,1)}, u32[]{:S(2)}, u32[]{:S(2)}) %collective-permute-start.66) | collective-permute-done | bytes 1048608 | tf_op jit(solution)/shard_map/ppermute | solution.py:413
  968.4 128.2 %collective-permute-done.69.refs_0_ = bf16[256,2048]{1,0:T(8,128)(2,1)S(1)} collective-permute-done((bf16[256,2048]{1,0:T(8,128)(2,1)}, bf16[256,2048]{1,0:T(8,128)(2,1)S(1)}, u32[]{:S(2)}, u32[]{:S(2)}) %collective-permute-start.69) | collective-permute-done | bytes 1048608 | tf_op jit(solution)/shard_map/ppermute | solution.py:413
  1120.5 10.1 shard_map.243.refs_3_
  1139.2 19.8 %collective-permute-done.72.refs_0_ = bf16[256,4096]{1,0:T(8,128)(2,1)} collective-permute-done((bf16[256,4096]{1,0:T(8,128)(2,1)}, bf16[256,4096]{1,0:T(8,128)(2,1)}, u32[]{:S(2)}, u32[]{:S(2)}) %collective-permute-start.72) | collective-permute-done | bytes 2097184 | tf_op jit(solution)/shard_map/ppermute | solution.py:404
  1180.8 10.9 fusion.3
  1219.3 18.9 %collective-permute-done.77.refs_0_ = bf16[64,4096]{1,0:T(8,128)(2,1)} collective-permute-done((bf16[64,4096]{1,0:T(8,128)(2,1)}, bf16[64,4096]{1,0:T(8,128)(2,1)}, u32[]{:S(2)}, u32[]{:S(2)}) %collective-permute-start.77) | collective-permute-done | bytes 524320 | tf_op jit(solution)/shard_map/ppermute | solution.py:408
  1238.2 15.2 collective-permute-done.78.refs_1_
  1255.2 11.4 collective-permute-start.88
  1287.4 12.7 collective-permute-done.83.refs_0_
  1300.2 15.7 collective-permute-done.84.refs_1_
  1317.7 9.5 collective-permute-start.96
  1387.2 12.4 convert_element_type.480
  1415.8 13.4 collective-permute-done.103.refs_6_
  1433.4 17.1 %collective-permute-done.98.refs_1_ = bf16[64,2048]{1,0:T(8,128)(2,1)S(1)} collective-permute-done((bf16[64,2048]{1,0:T(8,128)(2,1)S(1)}, bf16[64,2048]{1,0:T(8,128)(2,1)S(1)}, u32[]{:S(2)}, u32[]{:S(2)}) %collective-permute-start.98) | collective-permute-done | bytes 262176 | tf_op jit(solution)/shard_map/ppermute | solution.py:408
  1475.3 9.3 collective-permute-done.107.refs_2_
  1485.6 9.9 collective-permute-done.109.refs_4_
  1497.3 52.2 %all-gather.11.cloned.1.call-done.refs_6_ = bf16[512,16384]{1,0:T(8,128)(2,1)} async-done(((bf16[64,16384]{1,0:T(8,128)(2,1)}), bf16[512,16384]{1,0:T(8,128)(2,1)}) %all-gather.11.cloned.1.call-update) | async-done | bytes 16777232 | tf_op jit(solution)/shard_map/all_gather | solution.py:894
  1555.2 18.6 %slice_convert_fusion = (f32[512,8192]{1,0:T(8,128)}, f32[512,8192]{1,0:T(8,128)}) fusion(bf16[512,16384]{1,0:T(8,128)(2,1)} %get-tuple-element.382), kind=kLoop, calls=%fused_computation.1 | loop fusion | flops 8388608 | bytes 50331648 | tf_op jit(solution)/shard_map/convert_element_type | solution.py:910
  (926 shorter events, 744.4 us)
Async XLA Ops:
  7.2 223.4 %all-gather.5.cloned.1.call-start = ((), (), s32[]{:S(2)}) async-start(), calls=%async_computation.2 | async-start | bytes 9437184 | tf_op jit(solution)/shard_map/all_gather | solution.py:765
  28.9 50.3 %collective-permute-start.8 = (bf16[128,2048]{1,0:T(8,128)(2,1)}, bf16[128,2048]{1,0:T(8,128)(2,1)}, u32[]{:S(2)}, u32[]{:S(2)}) collective-permute-start(bf16[128,2048]{1,0:T(8,128)(2,1)} %get-tuple-element.467), channel_id=1, source_target_pairs={{0,1},{1,0},{2,3},{3,2},{4,5},{5,4},{6,7},{7,6},{8,9},{9,8},{10,11... | collective-permute-start | bytes 1572872 | tf_op jit(solution)/shard_map/ppermute | solution.py:404
  119.0 165.3 %all-gather.7.cloned.1.call-start = ((), (), s32[]{:S(2)}) async-start(), calls=%async_computation.3 | async-start | bytes 9437184 | tf_op jit(solution)/shard_map/all_gather | solution.py:765
  119.8 635.1 %reduce-scatter.3.cloned.1.call-start = ((), (), s32[]{:S(2)}) async-start(), calls=%async_computation.4 | async-start | bytes 9437184 | tf_op jit(solution)/shard_map/reduce_scatter | solution.py:831
  171.2 73.0 %collective-permute-start.31 = (bf16[256,2048]{1,0:T(8,128)(2,1)}, bf16[256,2048]{1,0:T(8,128)(2,1)}, u32[]{:S(2)}, u32[]{:S(2)}) collective-permute-start(bf16[256,2048]{1,0:T(8,128)(2,1)} %get-tuple-element.418), channel_id=1, source_target_pairs={{0,1},{1,0},{2,3},{3,2},{4,5},{5,4},{6,7},{7,6},{8,9},{9,8},{10,11... | collective-permute-start | bytes 3145736 | tf_op jit(solution)/shard_map/ppermute | solution.py:404
  186.4 59.2 %collective-permute-start.32 = (bf16[256,2048]{1,0:T(8,128)(2,1)}, bf16[256,2048]{1,0:T(8,128)(2,1)}, u32[]{:S(2)}, u32[]{:S(2)}) collective-permute-start(bf16[256,2048]{1,0:T(8,128)(2,1)} %get-tuple-element.417), channel_id=1, source_target_pairs={{0,2},{1,3},{2,0},{3,1},{4,6},{5,7},{6,4},{7,5},{8,10},{9,11},{10,... | collective-permute-start | bytes 3145736 | tf_op jit(solution)/shard_map/ppermute | solution.py:404
  188.4 58.6 %collective-permute-start.33 = (bf16[256,2048]{1,0:T(8,128)(2,1)}, bf16[256,2048]{1,0:T(8,128)(2,1)}, u32[]{:S(2)}, u32[]{:S(2)}) collective-permute-start(bf16[256,2048]{1,0:T(8,128)(2,1)} %get-tuple-element.416), channel_id=1, source_target_pairs={{0,3},{1,2},{2,1},{3,0},{4,7},{5,6},{6,5},{7,4},{8,11},{9,10},{10,... | collective-permute-start | bytes 3145736 | tf_op jit(solution)/shard_map/ppermute | solution.py:404
  189.0 58.7 %collective-permute-start.29 = (bf16[256,2048]{1,0:T(8,128)(2,1)}, bf16[256,2048]{1,0:T(8,128)(2,1)}, u32[]{:S(2)}, u32[]{:S(2)}) collective-permute-start(bf16[256,2048]{1,0:T(8,128)(2,1)} %get-tuple-element.213), channel_id=1, source_target_pairs={{0,4},{4,0},{8,12},{12,8},{16,20},{20,16},{24,28},{28,24},{1,5},{5... | collective-permute-start | bytes 3145736 | tf_op jit(solution)/shard_map/ppermute | solution.py:408
  189.1 60.2 %collective-permute-start.30 = (bf16[256,2048]{1,0:T(8,128)(2,1)}, bf16[256,2048]{1,0:T(8,128)(2,1)}, u32[]{:S(2)}, u32[]{:S(2)}) collective-permute-start(bf16[256,2048]{1,0:T(8,128)(2,1)} %get-tuple-element.214), channel_id=1, source_target_pairs={{0,4},{4,0},{8,12},{12,8},{16,20},{20,16},{24,28},{28,24},{1,5},{5... | collective-permute-start | bytes 3145736 | tf_op jit(solution)/shard_map/ppermute | solution.py:408
  244.3 56.8 %collective-permute-start.37 = (bf16[256,2048]{1,0:T(8,128)(2,1)}, bf16[256,2048]{1,0:T(8,128)(2,1)}, u32[]{:S(2)}, u32[]{:S(2)}) collective-permute-start(bf16[256,2048]{1,0:T(8,128)(2,1)} %get-tuple-element.415), channel_id=1, source_target_pairs={{0,1},{1,0},{2,3},{3,2},{4,5},{5,4},{6,7},{7,6},{8,9},{9,8},{10,11... | collective-permute-start | bytes 3145736 | tf_op jit(solution)/shard_map/ppermute | solution.py:404
  245.6 56.9 %collective-permute-start.38 = (bf16[256,2048]{1,0:T(8,128)(2,1)}, bf16[256,2048]{1,0:T(8,128)(2,1)}, u32[]{:S(2)}, u32[]{:S(2)}) collective-permute-start(bf16[256,2048]{1,0:T(8,128)(2,1)} %get-tuple-element.414), channel_id=1, source_target_pairs={{0,2},{1,3},{2,0},{3,1},{4,6},{5,7},{6,4},{7,5},{8,10},{9,11},{10,... | collective-permute-start | bytes 3145736 | tf_op jit(solution)/shard_map/ppermute | solution.py:404
  247.0 57.1 %collective-permute-start.39 = (bf16[256,2048]{1,0:T(8,128)(2,1)}, bf16[256,2048]{1,0:T(8,128)(2,1)}, u32[]{:S(2)}, u32[]{:S(2)}) collective-permute-start(bf16[256,2048]{1,0:T(8,128)(2,1)} %get-tuple-element.413), channel_id=1, source_target_pairs={{0,3},{1,2},{2,1},{3,0},{4,7},{5,6},{6,5},{7,4},{8,11},{9,10},{10,... | collective-permute-start | bytes 3145736 | tf_op jit(solution)/shard_map/ppermute | solution.py:404
  247.8 66.5 %collective-permute-start.40 = (bf16[256,2048]{1,0:T(8,128)(2,1)}, bf16[256,2048]{1,0:T(8,128)(2,1)}, u32[]{:S(2)}, u32[]{:S(2)}) collective-permute-start(bf16[256,2048]{1,0:T(8,128)(2,1)} %pad_maximum_fusion.14), channel_id=1, source_target_pairs={{0,2},{1,3},{2,0},{3,1},{4,6},{5,7},{6,4},{7,5},{8,10},{9,11},{10,... | collective-permute-start | bytes 3145736 | tf_op jit(solution)/shard_map/ppermute | solution.py:404
  249.3 70.4 %collective-permute-start.41 = (bf16[256,2048]{1,0:T(8,128)(2,1)}, bf16[256,2048]{1,0:T(8,128)(2,1)}, u32[]{:S(2)}, u32[]{:S(2)}) collective-permute-start(bf16[256,2048]{1,0:T(8,128)(2,1)} %pad_maximum_fusion.15), channel_id=1, source_target_pairs={{0,1},{1,0},{2,3},{3,2},{4,5},{5,4},{6,7},{7,6},{8,9},{9,8},{10,11... | collective-permute-start | bytes 3145736 | tf_op jit(solution)/shard_map/ppermute | solution.py:404
  442.1 77.7 %collective-permute-start.54 = (bf16[256,2048]{1,0:T(8,128)(2,1)}, bf16[256,2048]{1,0:T(8,128)(2,1)}, u32[]{:S(2)}, u32[]{:S(2)}) collective-permute-start(bf16[256,2048]{1,0:T(8,128)(2,1)} %pad_maximum_fusion.21), channel_id=1, source_target_pairs={{0,1},{1,0},{2,3},{3,2},{4,5},{5,4},{6,7},{7,6},{8,9},{9,8},{10,11... | collective-permute-start | bytes 3145736 | tf_op jit(solution)/shard_map/ppermute | solution.py:404
  445.1 74.8 %collective-permute-start.53 = (bf16[256,2048]{1,0:T(8,128)(2,1)}, bf16[256,2048]{1,0:T(8,128)(2,1)}, u32[]{:S(2)}, u32[]{:S(2)}) collective-permute-start(bf16[256,2048]{1,0:T(8,128)(2,1)} %pad_maximum_fusion.20), channel_id=1, source_target_pairs={{0,2},{1,3},{2,0},{3,1},{4,6},{5,7},{6,4},{7,5},{8,10},{9,11},{10,... | collective-permute-start | bytes 3145736 | tf_op jit(solution)/shard_map/ppermute | solution.py:404
  526.9 79.4 %collective-permute-start.55 = (bf16[256,2048]{1,0:T(8,128)(2,1)}, bf16[256,2048]{1,0:T(8,128)(2,1)}, u32[]{:S(2)}, u32[]{:S(2)}) collective-permute-start(bf16[256,2048]{1,0:T(8,128)(2,1)} %get-tuple-element.259), channel_id=1, source_target_pairs={{0,2},{1,3},{2,0},{3,1},{4,6},{5,7},{6,4},{7,5},{8,10},{9,11},{10,... | collective-permute-start | bytes 3145736 | tf_op jit(solution)/shard_map/ppermute | solution.py:404
  528.4 77.9 %collective-permute-start.56 = (bf16[256,2048]{1,0:T(8,128)(2,1)}, bf16[256,2048]{1,0:T(8,128)(2,1)}, u32[]{:S(2)}, u32[]{:S(2)}) collective-permute-start(bf16[256,2048]{1,0:T(8,128)(2,1)} %get-tuple-element.260), channel_id=1, source_target_pairs={{0,1},{1,0},{2,3},{3,2},{4,5},{5,4},{6,7},{7,6},{8,9},{9,8},{10,11... | collective-permute-start | bytes 3145736 | tf_op jit(solution)/shard_map/ppermute | solution.py:404
  648.7 206.9 %all-gather.9.cloned.1.call-start = ((), (), s32[]{:S(2)}) async-start(), calls=%async_computation.5 | async-start | bytes 9437184 | tf_op jit(solution)/shard_map/all_gather | solution.py:859
  754.9 561.0 %reduce-scatter.5.cloned.1.call-start = ((), (), s32[]{:S(2)}) async-start(), calls=%async_computation.6 | async-start | bytes 18874368 | tf_op jit(solution)/shard_map/reduce_scatter | solution.py:864
  780.7 74.9 %collective-permute-start.65 = (bf16[512,2048]{1,0:T(8,128)(2,1)}, bf16[512,2048]{1,0:T(8,128)(2,1)S(1)}, u32[]{:S(2)}, u32[]{:S(2)}) collective-permute-start(bf16[512,2048]{1,0:T(8,128)(2,1)} %get-tuple-element.299), channel_id=1, source_target_pairs={{0,4},{4,0},{8,12},{12,8},{16,20},{20,16},{24,28},{28,24},{1,5},{5... | collective-permute-start | bytes 6291464 | tf_op jit(solution)/shard_map/ppermute | solution.py:408
  785.4 70.2 %collective-permute-start.64 = (bf16[256,2048]{1,0:T(8,128)(2,1)}, bf16[256,2048]{1,0:T(8,128)(2,1)S(1)}, u32[]{:S(2)}, u32[]{:S(2)}) collective-permute-start(bf16[256,2048]{1,0:T(8,128)(2,1)} %get-tuple-element.298), channel_id=1, source_target_pairs={{0,8},{4,12},{8,0},{12,4},{16,24},{20,28},{24,16},{28,20},{1,9},{5... | collective-permute-start | bytes 3145736 | tf_op jit(solution)/shard_map/ppermute | solution.py:408
  857.3 692.2 %all-gather.11.cloned.1.call-start = ((), (), s32[]{:S(2)}) async-start(), calls=%async_computation.7 | async-start | bytes 18874368 | tf_op jit(solution)/shard_map/all_gather | solution.py:894
  872.5 81.3 %collective-permute-start.66 = (bf16[256,2048]{1,0:T(8,128)(2,1)}, bf16[256,2048]{1,0:T(8,128)(2,1)}, u32[]{:S(2)}, u32[]{:S(2)}) collective-permute-start(bf16[256,2048]{1,0:T(8,128)(2,1)} %get-tuple-element.305), channel_id=1, source_target_pairs={{16,0},{20,4},{24,8},{28,12},{17,1},{21,5},{25,9},{29,13},{18,2},{... | collective-permute-start | bytes 3145736 | tf_op jit(solution)/shard_map/ppermute | solution.py:413
  874.0 79.7 %collective-permute-start.67 = (bf16[256,2048]{1,0:T(8,128)(2,1)}, bf16[256,2048]{1,0:T(8,128)(2,1)}, u32[]{:S(2)}, u32[]{:S(2)}) collective-permute-start(bf16[256,2048]{1,0:T(8,128)(2,1)} %get-tuple-element.306), channel_id=1, source_target_pairs={{20,16},{24,20},{28,24},{21,17},{25,21},{29,25},{22,18},{26,22},{3... | collective-permute-start | bytes 3145736 | tf_op jit(solution)/shard_map/ppermute | solution.py:413
  875.7 78.1 %collective-permute-start.68 = (bf16[256,2048]{1,0:T(8,128)(2,1)}, bf16[256,2048]{1,0:T(8,128)(2,1)}, u32[]{:S(2)}, u32[]{:S(2)}) collective-permute-start(bf16[256,2048]{1,0:T(8,128)(2,1)} %get-tuple-element.307), channel_id=1, source_target_pairs={{0,8},{4,12},{8,0},{12,4},{16,24},{20,28},{24,16},{28,20},{1,9},{5... | collective-permute-start | bytes 3145736 | tf_op jit(solution)/shard_map/ppermute | solution.py:408
  965.5 131.2 %collective-permute-start.71 = (bf16[4,256,4096]{2,1,0:T(8,128)(2,1)}, bf16[4,256,4096]{2,1,0:T(8,128)(2,1)}, u32[]{:S(2)}, u32[]{:S(2)}) collective-permute-start(bf16[4,256,4096]{2,1,0:T(8,128)(2,1)} %get-tuple-element.315), channel_id=1, source_target_pairs={{0,4},{4,0},{8,12},{12,8},{16,20},{20,16},{24,28},{28,24},{1,5},{5... | collective-permute-start | bytes 25165832 | tf_op jit(solution)/shard_map/ppermute | solution.py:408
  965.5 131.1 %collective-permute-start.69 = (bf16[256,2048]{1,0:T(8,128)(2,1)}, bf16[256,2048]{1,0:T(8,128)(2,1)S(1)}, u32[]{:S(2)}, u32[]{:S(2)}) collective-permute-start(bf16[256,2048]{1,0:T(8,128)(2,1)} %get-tuple-element.313), channel_id=1, source_target_pairs={{16,0},{20,4},{24,8},{28,12},{17,1},{21,5},{25,9},{29,13},{18,2},{... | collective-permute-start | bytes 3145736 | tf_op jit(solution)/shard_map/ppermute | solution.py:413
  966.8 129.9 %collective-permute-start.70 = (bf16[256,2048]{1,0:T(8,128)(2,1)}, bf16[256,2048]{1,0:T(8,128)(2,1)}, u32[]{:S(2)}, u32[]{:S(2)}) collective-permute-start(bf16[256,2048]{1,0:T(8,128)(2,1)} %get-tuple-element.314), channel_id=1, source_target_pairs={{20,16},{24,20},{28,24},{21,17},{25,21},{29,25},{22,18},{26,22},{3... | collective-permute-start | bytes 3145736 | tf_op jit(solution)/shard_map/ppermute | solution.py:413
  1110.9 48.1 %collective-permute-start.72 = (bf16[256,4096]{1,0:T(8,128)(2,1)}, bf16[256,4096]{1,0:T(8,128)(2,1)}, u32[]{:S(2)}, u32[]{:S(2)}) collective-permute-start(bf16[256,4096]{1,0:T(8,128)(2,1)} %get-tuple-element.317), channel_id=1, source_target_pairs={{0,2},{1,3},{2,0},{3,1},{4,6},{5,7},{6,4},{7,5},{8,10},{9,11},{10,... | collective-permute-start | bytes 6291464 | tf_op jit(solution)/shard_map/ppermute | solution.py:404
  1112.4 47.8 %collective-permute-start.73 = (bf16[256,4096]{1,0:T(8,128)(2,1)}, bf16[256,4096]{1,0:T(8,128)(2,1)}, u32[]{:S(2)}, u32[]{:S(2)}) collective-permute-start(bf16[256,4096]{1,0:T(8,128)(2,1)} %get-tuple-element.318), channel_id=1, source_target_pairs={{0,1},{1,0},{2,3},{3,2},{4,5},{5,4},{6,7},{7,6},{8,9},{9,8},{10,11... | collective-permute-start | bytes 6291464 | tf_op jit(solution)/shard_map/ppermute | solution.py:404
  1386.1 47.0 %collective-permute-start.104 = (bf16[256,2048]{1,0:T(8,128)(2,1)}, bf16[256,2048]{1,0:T(8,128)(2,1)}, u32[]{:S(2)}, u32[]{:S(2)}) collective-permute-start(bf16[256,2048]{1,0:T(8,128)(2,1)} %get-tuple-element.360), channel_id=1, source_target_pairs={{0,1},{1,0},{2,3},{3,2},{4,5},{5,4},{6,7},{7,6},{8,9},{9,8},{10,11... | collective-permute-start | bytes 3145736 | tf_op jit(solution)/shard_map/ppermute | solution.py:404
  (273 other events, 5203.8 us)
Sparse Core Ops, SparseCore 0:
  119.1 82.3 all-gather.4
  203.7 80.5 all-gather.6
  648.8 105.9 reduce-scatter.2
  756.3 97.4 all-gather.8
  857.4 261.0 reduce-scatter.4
  1378.6 170.8 all-gather.10

commit v2 on v1

--- a/solution.py
+++ b/solution.py
@@ -827,8 +827,10 @@
     act, grad_wide = wide
 
     line.launch(*grad_flows)
-    down = line.settle(product(act, joined([f.result for f in gz])))
-    down_part = lax.psum_scatter(down, "ctx", scatter_dimension=0, tiled=True)
+    grad_up = line.settle(product(joined(b_all), grad_wide))
+    up_part = lax.psum_scatter(
+        grad_up.reshape(planes, shard, 2 * ff_own), "ctx", scatter_dimension=1, tiled=True
+    )
     line.launch(*grad_flows)
     line.settle()
     line.finish(*grad_flows)
@@ -850,65 +852,69 @@
         gq, *gkv = attend_back(
             flags[m], places, biases[m], queries, keys[m], mixed[m], grads_mixed[m], lses[m], cosine, sine, m, block
         )
-        if m == 0:
-            gq, *gkv, grads_mixed[-1], down_part = line.settle(gq, *gkv, grads_mixed[-1], down_part)
+        if m + 1 < batches:
+            gq, *gkv, grads_mixed[-1] = line.settle(gq, *gkv, grads_mixed[-1])
         else:
             gq, *gkv = line.settle(gq, *gkv)
         grads_q.append(gq)
         key_backs.append(Flow(keys_back_flow(*gkv), True))
-    down_all = lax.all_gather(down_part, "ctx", axis=0, tiled=True)
 
     gq = joined(grads_q)
     line.launch(*key_backs)
-    grad_up, down_all = line.settle(product(joined(b_all), grad_wide), down_all)
-    up_part = lax.psum_scatter(
-        grad_up.reshape(planes, shard, 2 * ff_own), "ctx", scatter_dimension=1, tiled=True
-    )
-    line.launch(*key_backs)
-    grad_attn = line.settle(product(jnp.stack([attn_in, joined(mixed)]), jnp.stack([gq, joined(gys)])))
+    grad_down = product(act, joined([f.result for f in gz]))
+    grad_attn = product(jnp.stack([attn_in, joined(mixed)]), jnp.stack([gq, joined(gys)]))
+    grad_down, grad_attn, up_part = line.settle(grad_down, grad_attn, up_part)
+    down_part = lax.psum_scatter(grad_down, "ctx", scatter_dimension=0, tiled=True)
     grad_attn = Flow(rows_flow(grad_attn), True)
+    up_line = Flow(exchange_flow(up_part, 2))
+    line.launch(*key_backs, grad_attn, up_line)
+    line.settle()
+    line.finish(up_line)
+    up_all = lax.all_gather(up_line.result, "ctx", axis=0, tiled=True)
     line.launch(*key_backs, grad_attn)
     line.settle()
     line.finish(*key_backs)
     line.launch(grad_attn)
     gkv = unturn(joined([f.result for f in key_backs]), cosine, sine)
-    grad_keys, gkv = line.settle(product(attn_in, gkv), gkv)
+    grad_keys, gkv, down_part = line.settle(product(attn_in, gkv), gkv, down_part)
     grad_keys = Flow(rows_flow(grad_keys), True)
-    line.launch(grad_attn, grad_keys)
+    line.finish(grad_attn)
+    line.launch(grad_keys)
     grad_attn_in = nt(gq, query_weight.result) + nt(gkv, keys_weight.result)
     grad_part, grad_attn_gain = norm_back(grad_attn_in, hidden, scaled_attn, inverse_attn, gain_attn)
     grad_in = (joined(grad_middles) + grad_part).astype(bf16)
-    gains_back = Flow(total_flow(line.settle(jnp.stack([grad_attn_gain, grad_ffn_gain]))))
-    line.finish(grad_attn)
-    attn_out = Flow(direct_flow(grad_attn.result, [qd, width]))
-    line.launch(attn_out, grad_keys, gains_back)
+    gain_grads, down_part = line.settle(jnp.stack([grad_attn_gain, grad_ffn_gain]), down_part)
+    gains_back = Flow(total_flow(gain_grads))
+    line.launch(grad_keys, gains_back)
+    down_part = line.settle(down_part)
+    down_all = lax.all_gather(down_part, "ctx", axis=0, tiled=True)
+    line.launch(grad_keys, gains_back)
     line.settle()
-    line.launch(attn_out, grad_keys, gains_back)
-    up_part = line.settle(up_part)
     line.finish(grad_keys)
-    keys_out = Flow(direct_flow(grad_keys.result, [kvd, kvd]))
-    up_line = Flow(exchange_flow(up_part, 2))
-    line.launch(up_line, attn_out, keys_out, gains_back)
-    line.settle()
-    line.finish(up_line)
-    up_all = lax.all_gather(up_line.result, "ctx", axis=0, tiled=True)
-    line.launch(keys_out, gains_back, *out_parts)
-    line.settle()
-    line.launch(keys_out, gains_back, *out_parts)
+    both = jnp.concatenate([grad_attn.result, grad_keys.result], axis=1)
+    attn_out = Flow(direct_flow(both, [qd, width, kvd, kvd]))
+    line.launch(attn_out, gains_back)
     up_all = line.settle(up_all)
-    line.finish(attn_out, keys_out, gains_back, *out_parts)
+    grad_gate = up_all[:, : planes * ff_own].astype(f32)
+    grad_up = up_all[:, planes * ff_own :].astype(f32)
+    line.launch(attn_out, gains_back, *out_parts)
+    grad_gate, grad_up, down_all = line.settle(grad_gate, grad_up, down_all)
+    grad_down = down_all.astype(f32)
+    line.launch(attn_out, gains_back, *out_parts)
+    grad_down = line.settle(grad_down)
+    line.finish(attn_out, gains_back, *out_parts)
     gain_grads = lax.dynamic_slice(gains_back.result, (0, me * shard), (2, shard))
     outputs = [(middles[m] + out_parts[m].result).astype(bf16) for m in groups]
     return (
         jnp.stack(outputs),
         grad_in.reshape(batches, block, width),
         attn_out.result[0],
-        keys_out.result[0],
-        keys_out.result[1],
+        attn_out.result[2],
+        attn_out.result[3],
         attn_out.result[1],
-        up_all[:, : planes * ff_own].astype(f32),
-        up_all[:, planes * ff_own :].astype(f32),
-        down_all.astype(f32),
+        grad_gate,
+        grad_up,
+        grad_down,
         gain_grads[0],
         gain_grads[1],
     )

time: 1600 us -> 1530 us (0.956)
  waiting for transfers between devices: 581 us -> 513 us
  local copies, waits for them, and re-layouts: 324 us -> 308 us
    all_gather x1, waiting for transfers between devices: 52.2 us -> 0.01 us  [local(): up_all = lax.all_gather(up_line.result, 'ctx', axis=0, tiled=True)]
    reduce_scatter x1, waiting for transfers between devices: 49 us -> 0.01 us  [local(): lax.psum_scatter(grad_down, 'ctx', scatter_dimension=0, tiled=True)]
    ppermute x41 -> x34, waiting for transfers between devices: 115 us -> 156 us  [cswap(): lax.ppermute(value, 'ctx', [(i, i ^ bits) for i in range(lax.axis_size('c...]
    unnamed x413 -> x347, local copies, waits for them, and re-layouts: 123 us -> 100 us
    ppermute x4, waiting for transfers between devices: 182 us -> 164 us  [move(): return lambda value: lax.ppermute(value, 'ctx', pairs)]
    ppermute x41 -> x34, starting transfers between devices: 68.2 us -> 56.8 us  [cswap(): lax.ppermute(value, 'ctx', [(i, i ^ bits) for i in range(lax.axis_size('c...]
    concatenate x23 -> x21, other arithmetic: 35.9 us -> 32.8 us  [joined(): return jnp.concatenate(parts, axis=0) if len(parts) > 1 else parts[0]]
    dynamic_update_slice x46 -> x42, local copies, waits for them, and re-layouts: 81.2 us -> 78.6 us  [put_rows(): return lax.dynamic_update_slice_in_dim(target, value, start, axis=0)]
  transfers between devices with their start and end apart: 117 -> 110, of which waited for: 41 -> 33; matrix products, arithmetic and copies ran while one was open for 25% -> 28% of each run, Pallas kernels for 18% -> 19%
where the time goes in v2:
time: 1530 us; the launch traced here: 1510 us
  waiting for transfers between devices  513 us (34%)
  local copies, waits for them, and re-layouts  308 us (20%)
  Pallas kernels  288 us (19%)
  other arithmetic  195 us (13%)
  starting transfers between devices  139 us (9%)
  matrix products  47.2 us (3%)
  between operations  16.6 us (1%)
    ppermute x4, waiting for transfers between devices, move(): return lambda value: lax.ppermute(value, 'ctx', pairs)  164 us
    ppermute x66, waiting for transfers between devices, fswap(): lax.ppermute(value, 'fsdp', [(i, i ^ bits) for i in range(plane())])  159 us
    ppermute x34, waiting for transfers between devices, cswap(): lax.ppermute(value, 'ctx', [(i, i ^ bits) for i in range(lax.axis_size('c...  156 us
    pallas_call x2, Pallas kernels, feed_forward(): pl.pallas_call(kernel, out_shape=(wide, jax.ShapeDtypeStruct((2,) + wide....  135 us
    unnamed x347, local copies, waits for them, and re-layouts  100 us
    pallas_call x4, Pallas kernels, product(): pl.pallas_call(product_kernel, out_shape=jax.ShapeDtypeStruct((count, sta...  86.9 us
    dynamic_update_slice x42, local copies, waits for them, and re-layouts, put_rows(): return lax.dynamic_update_slice_in_dim(target, value, start, axis=0)  78.6 us
    ppermute x66, starting transfers between devices, fswap(): lax.ppermute(value, 'fsdp', [(i, i ^ bits) for i in range(plane())])  75.1 us
  transfers between devices with their start and end apart: 110, of which 33 were waited for; matrix products, arithmetic and copies ran while one was open for 28% of the time, Pallas kernels for 19%

profile of v2, /device:TPU:0, one launch (start us, length us, event | category | flops | bytes accessed | tf_op | source)
XLA Modules:
  0.0 1506.7 jit_solution(6315402007242580408)
XLA Ops:
  53.6 16.4 %collective-permute-done.5.refs_3_ = bf16[256,2048]{1,0:T(8,128)(2,1)} collective-permute-done((bf16[256,2048]{1,0:T(8,128)(2,1)}, bf16[256,2048]{1,0:T(8,128)(2,1)}, u32[]{:S(2)}, u32[]{:S(2)}) %collective-permute-start.5) | collective-permute-done | bytes 1048608 | tf_op jit(solution)/shard_map/ppermute | solution.py:404
  103.6 8.8 shard_map.207.refs_6_
  173.6 13.8 collective-permute-done.23.refs_4_
  217.3 8.8 shard_map.211.q_ref
  261.2 24.0 %all-gather.7.cloned.1.call-done.kv_ref = bf16[2048,2048]{1,0:T(8,128)(2,1)} async-done(((bf16[256,2048]{1,0:T(8,128)(2,1)}), bf16[2048,2048]{1,0:T(8,128)(2,1)}) %all-gather.7.cloned.1.call-update) | async-done | bytes 8388624 | tf_op jit(solution)/shard_map/all_gather | solution.py:765
  413.8 16.5 %collective-permute-done.50.refs_1_ = bf16[256,2048]{1,0:T(8,128)(2,1)} collective-permute-done((bf16[256,2048]{1,0:T(8,128)(2,1)S(1)}, bf16[256,2048]{1,0:T(8,128)(2,1)}, u32[]{:S(2)}, u32[]{:S(2)}) %collective-permute-start.50) | collective-permute-done | bytes 1048608 | tf_op jit(solution)/shard_map/ppermute | solution.py:404
  450.5 67.8 %shard_map.220 = (bf16[2048,2048]{1,0:T(8,128)(2,1)}, bf16[2,2048,2048]{2,1,0:T(8,128)(2,1)}, bf16[1024,2048]{1,0:T(8,128)(2,1)}, bf16[1024,2048]{1,0:T(8,128)(2,1)}) custom-call(bf16[1024,2048]{1,0:T(8,128)(2,1)} %get-tuple-element.473.refs_0_, bf16[1,1024,2048]{2,1,0:T(8,128)(2,1)} %bitcast.168, ...), custom_call_target="tpu_custom_call" | custom-call | tf_op jit(solution)/shard_map/pallas_call | solution.py:375
  540.1 67.5 %shard_map.223 = (bf16[2048,2048]{1,0:T(8,128)(2,1)}, bf16[2,2048,2048]{2,1,0:T(8,128)(2,1)}, bf16[1024,2048]{1,0:T(8,128)(2,1)}, bf16[1024,2048]{1,0:T(8,128)(2,1)}) custom-call(bf16[1024,2048]{1,0:T(8,128)(2,1)} %get-tuple-element.469.refs_0_, bf16[1,1024,2048]{2,1,0:T(8,128)(2,1)} %bitcast.167, ...), custom_call_target="tpu_custom_call", output_to_operand_aliasing={{0}: (5, {}), {1}: (6, {})} | custom-call | tf_op jit(solution)/shard_map/pallas_call | solution.py:375
  618.7 41.3 %shard_map.226.refs_4_ = bf16[2048,4096]{1,0:T(8,128)(2,1)} custom-call(bf16[1,2048,2048]{2,1,0:T(8,128)(2,1)} %bitcast.26.left_ref, bf16[2,2048,2048]{2,1,0:T(8,128)(2,1)} %get-tuple-element.273.right_ref), custom_call_target="tpu_custom_call" | custom-call | tf_op jit(solution)/shard_map/pallas_call | solution.py:86
  695.0 11.4 shard_map.228
  706.4 9.4 convolution_convert_fusion.refs_3_
  718.6 11.6 shard_map.232
  748.9 23.3 %shard_map.235.refs_2_ = bf16[2048,2048]{1,0:T(8,128)(2,1)} custom-call(bf16[1,2048,2048]{2,1,0:T(8,128)(2,1)} %bitcast.162, bf16[1,2048,2048]{2,1,0:T(8,128)(2,1)} %bitcast.166), custom_call_target="tpu_custom_call" | custom-call | tf_op jit(solution)/shard_map/pallas_call | solution.py:86
  772.2 29.0 %collective-permute-start.64 = (bf16[256,2048]{1,0:T(8,128)(2,1)S(1)}, bf16[256,2048]{1,0:T(8,128)(2,1)S(1)}, u32[]{:S(2)}, u32[]{:S(2)}) collective-permute-start(bf16[256,2048]{1,0:T(8,128)(2,1)S(1)} %copy-done.106), channel_id=1, source_target_pairs={{0,8},{4,12},{8,0},{12,4},{16,24},{20,28},{24,16},{28,20},{1,9},{5... | collective-permute-start | bytes 3145736 | tf_op jit(solution)/shard_map/ppermute | solution.py:408
  804.4 15.4 %shard_map.236.refs_3_ = bf16[2048,4096]{1,0:T(8,128)(2,1)} custom-call(bf16[2,512,2048]{2,1,0:T(8,128)(2,1)S(1)} %pad_maximum_fusion.left_ref, bf16[2,512,2048]{2,1,0:T(8,128)(2,1)} %pad_maximum_fusion.1.right_ref), custom_call_target="tpu_custom_call" | custom-call | tf_op jit(solution)/shard_map/pallas_call | solution.py:86
  819.8 33.7 %collective-permute-done.64.refs_0_ = bf16[256,2048]{1,0:T(8,128)(2,1)S(1)} collective-permute-done((bf16[256,2048]{1,0:T(8,128)(2,1)S(1)}, bf16[256,2048]{1,0:T(8,128)(2,1)S(1)}, u32[]{:S(2)}, u32[]{:S(2)}) %collective-permute-start.64) | collective-permute-done | bytes 1048608 | tf_op jit(solution)/shard_map/ppermute | solution.py:408
  853.6 9.6 reduce-scatter.3.cloned.1.call-done.refs_4_
  872.3 8.2 constant_dynamic-slice_fusion.9.refs_3_
  902.8 12.2 collective-permute-done.72.refs_6_
  915.0 52.6 %collective-permute-done.66.refs_0_ = bf16[256,2048]{1,0:T(8,128)(2,1)} collective-permute-done((bf16[256,2048]{1,0:T(8,128)(2,1)}, bf16[256,2048]{1,0:T(8,128)(2,1)}, u32[]{:S(2)}, u32[]{:S(2)}) %collective-permute-start.66) | collective-permute-done | bytes 1048608 | tf_op jit(solution)/shard_map/ppermute | solution.py:413
  1012.3 111.1 %collective-permute-done.73.refs_0_ = bf16[256,2048]{1,0:T(8,128)(2,1)} collective-permute-done((bf16[256,2048]{1,0:T(8,128)(2,1)}, bf16[256,2048]{1,0:T(8,128)(2,1)}, u32[]{:S(2)}, u32[]{:S(2)}) %collective-permute-start.73) | collective-permute-done | bytes 1048608 | tf_op jit(solution)/shard_map/ppermute | solution.py:413
  1143.0 10.2 shard_map.243.refs_3_
  1166.8 9.6 fusion.35
  1176.5 8.5 fusion.3
  1197.3 23.2 %collective-permute-done.80.refs_0_ = bf16[256,2048]{1,0:T(8,128)(2,1)S(1)} collective-permute-done((bf16[256,2048]{1,0:T(8,128)(2,1)}, bf16[256,2048]{1,0:T(8,128)(2,1)S(1)}, u32[]{:S(2)}, u32[]{:S(2)}) %collective-permute-start.80) | collective-permute-done | bytes 1048608 | tf_op jit(solution)/shard_map/ppermute | solution.py:404
  1235.1 9.4 collective-permute-done.83.refs_0_
  1247.6 9.8 maximum_maximum_fusion
  1267.7 98.9 %collective-permute-done.89.refs_3_ = f32[2,2048]{1,0:T(2,128)S(1)} collective-permute-done((f32[2,2048]{1,0:T(2,128)S(1)}, f32[2,2048]{1,0:T(2,128)S(1)}, u32[]{:S(2)}, u32[]{:S(2)}) %collective-permute-start.89) | collective-permute-done | bytes 16416 | tf_op jit(solution)/shard_map/ppermute | solution.py:408
  1375.4 17.6 %collective-permute-done.95.refs_5_ = bf16[256,2048]{1,0:T(8,128)(2,1)} collective-permute-done((bf16[256,2048]{1,0:T(8,128)(2,1)}, bf16[256,2048]{1,0:T(8,128)(2,1)}, u32[]{:S(2)}, u32[]{:S(2)}) %collective-permute-start.95) | collective-permute-done | bytes 1048608 | tf_op jit(solution)/shard_map/ppermute | solution.py:404
  1395.4 16.9 %slice_convert_fusion = (f32[512,8192]{1,0:T(8,128)}, f32[512,8192]{1,0:T(8,128)}) fusion(bf16[512,16384]{1,0:T(8,128)(2,1)} %get-tuple-element.355), kind=kLoop, calls=%fused_computation.1 | loop fusion | flops 8388608 | bytes 50331648 | tf_op jit(solution)/shard_map/convert_element_type | solution.py:899
  1414.0 15.5 %collective-permute-done.91.refs_1_ = bf16[64,6144]{1,0:T(8,128)(2,1)} collective-permute-done((bf16[64,6144]{1,0:T(8,128)(2,1)}, bf16[64,6144]{1,0:T(8,128)(2,1)}, u32[]{:S(2)}, u32[]{:S(2)}) %collective-permute-start.91) | collective-permute-done | bytes 786464 | tf_op jit(solution)/shard_map/ppermute | solution.py:408
  1457.9 11.7 convert_element_type.445.refs_6_
  (839 shorter events, 666.4 us)
Async XLA Ops:
  7.2 224.4 %all-gather.5.cloned.1.call-start = ((), (), s32[]{:S(2)}) async-start(), calls=%async_computation.2 | async-start | bytes 9437184 | tf_op jit(solution)/shard_map/all_gather | solution.py:765
  119.9 165.3 %all-gather.7.cloned.1.call-start = ((), (), s32[]{:S(2)}) async-start(), calls=%async_computation.3 | async-start | bytes 9437184 | tf_op jit(solution)/shard_map/all_gather | solution.py:765
  120.7 742.5 %reduce-scatter.3.cloned.1.call-start = ((), (), s32[]{:S(2)}) async-start(), calls=%async_computation.4 | async-start | bytes 18874368 | tf_op jit(solution)/shard_map/reduce_scatter | solution.py:831
  172.2 73.0 %collective-permute-start.31 = (bf16[256,2048]{1,0:T(8,128)(2,1)}, bf16[256,2048]{1,0:T(8,128)(2,1)}, u32[]{:S(2)}, u32[]{:S(2)}) collective-permute-start(bf16[256,2048]{1,0:T(8,128)(2,1)} %get-tuple-element.412), channel_id=1, source_target_pairs={{0,1},{1,0},{2,3},{3,2},{4,5},{5,4},{6,7},{7,6},{8,9},{9,8},{10,11... | collective-permute-start | bytes 3145736 | tf_op jit(solution)/shard_map/ppermute | solution.py:404
  187.4 59.2 %collective-permute-start.32 = (bf16[256,2048]{1,0:T(8,128)(2,1)}, bf16[256,2048]{1,0:T(8,128)(2,1)}, u32[]{:S(2)}, u32[]{:S(2)}) collective-permute-start(bf16[256,2048]{1,0:T(8,128)(2,1)} %get-tuple-element.411), channel_id=1, source_target_pairs={{0,2},{1,3},{2,0},{3,1},{4,6},{5,7},{6,4},{7,5},{8,10},{9,11},{10,... | collective-permute-start | bytes 3145736 | tf_op jit(solution)/shard_map/ppermute | solution.py:404
  189.4 58.8 %collective-permute-start.33 = (bf16[256,2048]{1,0:T(8,128)(2,1)}, bf16[256,2048]{1,0:T(8,128)(2,1)}, u32[]{:S(2)}, u32[]{:S(2)}) collective-permute-start(bf16[256,2048]{1,0:T(8,128)(2,1)} %get-tuple-element.410), channel_id=1, source_target_pairs={{0,3},{1,2},{2,1},{3,0},{4,7},{5,6},{6,5},{7,4},{8,11},{9,10},{10,... | collective-permute-start | bytes 3145736 | tf_op jit(solution)/shard_map/ppermute | solution.py:404
  190.0 58.7 %collective-permute-start.29 = (bf16[256,2048]{1,0:T(8,128)(2,1)}, bf16[256,2048]{1,0:T(8,128)(2,1)}, u32[]{:S(2)}, u32[]{:S(2)}) collective-permute-start(bf16[256,2048]{1,0:T(8,128)(2,1)} %get-tuple-element.210), channel_id=1, source_target_pairs={{0,4},{4,0},{8,12},{12,8},{16,20},{20,16},{24,28},{28,24},{1,5},{5... | collective-permute-start | bytes 3145736 | tf_op jit(solution)/shard_map/ppermute | solution.py:408
  190.1 60.1 %collective-permute-start.30 = (bf16[256,2048]{1,0:T(8,128)(2,1)}, bf16[256,2048]{1,0:T(8,128)(2,1)}, u32[]{:S(2)}, u32[]{:S(2)}) collective-permute-start(bf16[256,2048]{1,0:T(8,128)(2,1)} %get-tuple-element.211), channel_id=1, source_target_pairs={{0,4},{4,0},{8,12},{12,8},{16,20},{20,16},{24,28},{28,24},{1,5},{5... | collective-permute-start | bytes 3145736 | tf_op jit(solution)/shard_map/ppermute | solution.py:408
  248.7 66.5 %collective-permute-start.40 = (bf16[256,2048]{1,0:T(8,128)(2,1)}, bf16[256,2048]{1,0:T(8,128)(2,1)}, u32[]{:S(2)}, u32[]{:S(2)}) collective-permute-start(bf16[256,2048]{1,0:T(8,128)(2,1)} %pad_maximum_fusion.14), channel_id=1, source_target_pairs={{0,2},{1,3},{2,0},{3,1},{4,6},{5,7},{6,4},{7,5},{8,10},{9,11},{10,... | collective-permute-start | bytes 3145736 | tf_op jit(solution)/shard_map/ppermute | solution.py:404
  250.2 70.6 %collective-permute-start.41 = (bf16[256,2048]{1,0:T(8,128)(2,1)}, bf16[256,2048]{1,0:T(8,128)(2,1)}, u32[]{:S(2)}, u32[]{:S(2)}) collective-permute-start(bf16[256,2048]{1,0:T(8,128)(2,1)} %pad_maximum_fusion.15), channel_id=1, source_target_pairs={{0,1},{1,0},{2,3},{3,2},{4,5},{5,4},{6,7},{7,6},{8,9},{9,8},{10,11... | collective-permute-start | bytes 3145736 | tf_op jit(solution)/shard_map/ppermute | solution.py:404
  443.4 77.7 %collective-permute-start.54 = (bf16[256,2048]{1,0:T(8,128)(2,1)}, bf16[256,2048]{1,0:T(8,128)(2,1)}, u32[]{:S(2)}, u32[]{:S(2)}) collective-permute-start(bf16[256,2048]{1,0:T(8,128)(2,1)} %pad_maximum_fusion.21), channel_id=1, source_target_pairs={{0,1},{1,0},{2,3},{3,2},{4,5},{5,4},{6,7},{7,6},{8,9},{9,8},{10,11... | collective-permute-start | bytes 3145736 | tf_op jit(solution)/shard_map/ppermute | solution.py:404
  446.0 75.0 %collective-permute-start.53 = (bf16[256,2048]{1,0:T(8,128)(2,1)}, bf16[256,2048]{1,0:T(8,128)(2,1)}, u32[]{:S(2)}, u32[]{:S(2)}) collective-permute-start(bf16[256,2048]{1,0:T(8,128)(2,1)} %pad_maximum_fusion.20), channel_id=1, source_target_pairs={{0,2},{1,3},{2,0},{3,1},{4,6},{5,7},{6,4},{7,5},{8,10},{9,11},{10,... | collective-permute-start | bytes 3145736 | tf_op jit(solution)/shard_map/ppermute | solution.py:404
  528.1 79.6 %collective-permute-start.55 = (bf16[256,2048]{1,0:T(8,128)(2,1)}, bf16[256,2048]{1,0:T(8,128)(2,1)}, u32[]{:S(2)}, u32[]{:S(2)}) collective-permute-start(bf16[256,2048]{1,0:T(8,128)(2,1)} %get-tuple-element.256), channel_id=1, source_target_pairs={{0,2},{1,3},{2,0},{3,1},{4,6},{5,7},{6,4},{7,5},{8,10},{9,11},{10,... | collective-permute-start | bytes 3145736 | tf_op jit(solution)/shard_map/ppermute | solution.py:404
  529.6 78.1 %collective-permute-start.56 = (bf16[256,2048]{1,0:T(8,128)(2,1)}, bf16[256,2048]{1,0:T(8,128)(2,1)}, u32[]{:S(2)}, u32[]{:S(2)}) collective-permute-start(bf16[256,2048]{1,0:T(8,128)(2,1)} %get-tuple-element.257), channel_id=1, source_target_pairs={{0,1},{1,0},{2,3},{3,2},{4,5},{5,4},{6,7},{7,6},{8,9},{9,8},{10,11... | collective-permute-start | bytes 3145736 | tf_op jit(solution)/shard_map/ppermute | solution.py:404
  660.8 501.0 %reduce-scatter.5.cloned.1.call-start = ((), (), s32[]{:S(2)}) async-start(), calls=%async_computation.5 | async-start | bytes 9437184 | tf_op jit(solution)/shard_map/reduce_scatter | solution.py:867
  741.0 112.6 %collective-permute-start.65 = (bf16[512,2048]{1,0:T(8,128)(2,1)}, bf16[512,2048]{1,0:T(8,128)(2,1)}, u32[]{:S(2)}, u32[]{:S(2)}) collective-permute-start(bf16[512,2048]{1,0:T(8,128)(2,1)} %get-tuple-element.295), channel_id=1, source_target_pairs={{0,4},{4,0},{8,12},{12,8},{16,20},{20,16},{24,28},{28,24},{1,5},{5... | collective-permute-start | bytes 6291464 | tf_op jit(solution)/shard_map/ppermute | solution.py:408
  772.2 81.4 %collective-permute-start.64 = (bf16[256,2048]{1,0:T(8,128)(2,1)S(1)}, bf16[256,2048]{1,0:T(8,128)(2,1)S(1)}, u32[]{:S(2)}, u32[]{:S(2)}) collective-permute-start(bf16[256,2048]{1,0:T(8,128)(2,1)S(1)} %copy-done.106), channel_id=1, source_target_pairs={{0,8},{4,12},{8,0},{12,4},{16,24},{20,28},{24,16},{28,20},{1,9},{5... | collective-permute-start | bytes 3145736 | tf_op jit(solution)/shard_map/ppermute | solution.py:408
  863.2 506.9 %all-gather.9.cloned.1.call-start = ((), (), s32[]{:S(2)}) async-start(), calls=%async_computation.6 | async-start | bytes 18874368 | tf_op jit(solution)/shard_map/all_gather | solution.py:873
  880.4 93.7 %collective-permute-start.69 = (bf16[4,256,4096]{2,1,0:T(8,128)(2,1)}, bf16[4,256,4096]{2,1,0:T(8,128)(2,1)}, u32[]{:S(2)}, u32[]{:S(2)}) collective-permute-start(bf16[4,256,4096]{2,1,0:T(8,128)(2,1)} %get-tuple-element.307), channel_id=1, source_target_pairs={{0,4},{4,0},{8,12},{12,8},{16,20},{20,16},{24,28},{28,24},{1,5},{5... | collective-permute-start | bytes 25165832 | tf_op jit(solution)/shard_map/ppermute | solution.py:408
  886.2 81.4 %collective-permute-start.66 = (bf16[256,2048]{1,0:T(8,128)(2,1)}, bf16[256,2048]{1,0:T(8,128)(2,1)}, u32[]{:S(2)}, u32[]{:S(2)}) collective-permute-start(bf16[256,2048]{1,0:T(8,128)(2,1)} %get-tuple-element.304), channel_id=1, source_target_pairs={{16,0},{20,4},{24,8},{28,12},{17,1},{21,5},{25,9},{29,13},{18,2},{... | collective-permute-start | bytes 3145736 | tf_op jit(solution)/shard_map/ppermute | solution.py:413
  889.0 78.5 %collective-permute-start.67 = (bf16[256,2048]{1,0:T(8,128)(2,1)}, bf16[256,2048]{1,0:T(8,128)(2,1)}, u32[]{:S(2)}, u32[]{:S(2)}) collective-permute-start(bf16[256,2048]{1,0:T(8,128)(2,1)} %get-tuple-element.305), channel_id=1, source_target_pairs={{20,16},{24,20},{28,24},{21,17},{25,21},{29,25},{22,18},{26,22},{3... | collective-permute-start | bytes 3145736 | tf_op jit(solution)/shard_map/ppermute | solution.py:413
  898.6 75.5 %collective-permute-start.68 = (bf16[256,2048]{1,0:T(8,128)(2,1)}, bf16[256,2048]{1,0:T(8,128)(2,1)}, u32[]{:S(2)}, u32[]{:S(2)}) collective-permute-start(bf16[256,2048]{1,0:T(8,128)(2,1)} %get-tuple-element.306), channel_id=1, source_target_pairs={{0,8},{4,12},{8,0},{12,4},{16,24},{20,28},{24,16},{28,20},{1,9},{5... | collective-permute-start | bytes 3145736 | tf_op jit(solution)/shard_map/ppermute | solution.py:408
  987.7 426.2 %all-gather.11.cloned.1.call-start = ((), (), s32[]{:S(2)}) async-start(), calls=%async_computation.7 | async-start | bytes 9437184 | tf_op jit(solution)/shard_map/all_gather | solution.py:890
  1006.4 117.1 %collective-permute-start.75 = (bf16[256,4096]{1,0:T(8,128)(2,1)}, bf16[256,4096]{1,0:T(8,128)(2,1)}, u32[]{:S(2)}, u32[]{:S(2)}) collective-permute-start(bf16[256,4096]{1,0:T(8,128)(2,1)} %get-tuple-element.314), channel_id=1, source_target_pairs={{0,2},{1,3},{2,0},{3,1},{4,6},{5,7},{6,4},{7,5},{8,10},{9,11},{10,... | collective-permute-start | bytes 6291464 | tf_op jit(solution)/shard_map/ppermute | solution.py:404
  1008.2 115.3 %collective-permute-start.76 = (bf16[256,4096]{1,0:T(8,128)(2,1)}, bf16[256,4096]{1,0:T(8,128)(2,1)}, u32[]{:S(2)}, u32[]{:S(2)}) collective-permute-start(bf16[256,4096]{1,0:T(8,128)(2,1)} %get-tuple-element.315), channel_id=1, source_target_pairs={{0,1},{1,0},{2,3},{3,2},{4,5},{5,4},{6,7},{7,6},{8,9},{9,8},{10,11... | collective-permute-start | bytes 6291464 | tf_op jit(solution)/shard_map/ppermute | solution.py:404
  1009.4 114.1 %collective-permute-start.73 = (bf16[256,2048]{1,0:T(8,128)(2,1)}, bf16[256,2048]{1,0:T(8,128)(2,1)}, u32[]{:S(2)}, u32[]{:S(2)}) collective-permute-start(bf16[256,2048]{1,0:T(8,128)(2,1)} %get-tuple-element.312), channel_id=1, source_target_pairs={{16,0},{20,4},{24,8},{28,12},{17,1},{21,5},{25,9},{29,13},{18,2},{... | collective-permute-start | bytes 3145736 | tf_op jit(solution)/shard_map/ppermute | solution.py:413
  1010.7 112.8 %collective-permute-start.74 = (bf16[256,2048]{1,0:T(8,128)(2,1)}, bf16[256,2048]{1,0:T(8,128)(2,1)}, u32[]{:S(2)}, u32[]{:S(2)}) collective-permute-start(bf16[256,2048]{1,0:T(8,128)(2,1)} %get-tuple-element.313), channel_id=1, source_target_pairs={{20,16},{24,20},{28,24},{21,17},{25,21},{29,25},{22,18},{26,22},{3... | collective-permute-start | bytes 3145736 | tf_op jit(solution)/shard_map/ppermute | solution.py:413
  1258.9 109.2 %collective-permute-start.86 = (bf16[64,6144]{1,0:T(8,128)(2,1)}, bf16[64,6144]{1,0:T(8,128)(2,1)S(1)}, u32[]{:S(2)}, u32[]{:S(2)}) collective-permute-start(bf16[64,6144]{1,0:T(8,128)(2,1)} %get-tuple-element.439), channel_id=1, source_target_pairs={{0,8},{4,12},{8,0},{12,4},{16,24},{20,28},{24,16},{28,20},{1,9},{5... | collective-permute-start | bytes 2359304 | tf_op jit(solution)/shard_map/ppermute | solution.py:408
  1260.7 108.9 %collective-permute-start.87 = (bf16[64,6144]{1,0:T(8,128)(2,1)}, bf16[64,6144]{1,0:T(8,128)(2,1)}, u32[]{:S(2)}, u32[]{:S(2)}) collective-permute-start(bf16[64,6144]{1,0:T(8,128)(2,1)} %get-tuple-element.438), channel_id=1, source_target_pairs={{0,16},{4,20},{8,24},{12,28},{16,0},{20,4},{24,8},{28,12},{1,17},{... | collective-permute-start | bytes 2359304 | tf_op jit(solution)/shard_map/ppermute | solution.py:408
  1260.7 109.5 %collective-permute-start.88 = (bf16[64,6144]{1,0:T(8,128)(2,1)}, bf16[64,6144]{1,0:T(8,128)(2,1)}, u32[]{:S(2)}, u32[]{:S(2)}) collective-permute-start(bf16[64,6144]{1,0:T(8,128)(2,1)} %get-tuple-element.437), channel_id=1, source_target_pairs={{0,24},{4,28},{8,16},{12,20},{16,8},{20,12},{24,0},{28,4},{1,25},{... | collective-permute-start | bytes 2359304 | tf_op jit(solution)/shard_map/ppermute | solution.py:408
  1264.8 101.9 %collective-permute-start.89 = (f32[2,2048]{1,0:T(2,128)S(1)}, f32[2,2048]{1,0:T(2,128)S(1)}, u32[]{:S(2)}, u32[]{:S(2)}) collective-permute-start(f32[2,2048]{1,0:T(2,128)S(1)} %add.732), channel_id=1, source_target_pairs={{0,16},{4,20},{8,24},{12,28},{16,0},{20,4},{24,8},{28,12},{1,17},{... | collective-permute-start | bytes 49160 | tf_op jit(solution)/shard_map/ppermute | solution.py:408
  1266.6 107.4 %collective-permute-start.94 = (bf16[256,2048]{1,0:T(8,128)(2,1)}, bf16[256,2048]{1,0:T(8,128)(2,1)}, u32[]{:S(2)}, u32[]{:S(2)}) collective-permute-start(bf16[256,2048]{1,0:T(8,128)(2,1)} %get-tuple-element.351), channel_id=1, source_target_pairs={{0,2},{1,3},{2,0},{3,1},{4,6},{5,7},{6,4},{7,5},{8,10},{9,11},{10,... | collective-permute-start | bytes 3145736 | tf_op jit(solution)/shard_map/ppermute | solution.py:404
  (233 other events, 4768.8 us)
Sparse Core Ops, SparseCore 0:
  120.1 82.3 all-gather.4
  204.6 80.5 all-gather.6
  660.9 202.2 reduce-scatter.2
  865.4 143.7 reduce-scatter.4
  1010.6 189.5 all-gather.8
  1221.6 130.2 all-gather.10

commit v3 on v2

--- a/solution.py
+++ b/solution.py
@@ -860,7 +860,7 @@
         key_backs.append(Flow(keys_back_flow(*gkv), True))
 
     gq = joined(grads_q)
-    line.launch(*key_backs)
+    line.launch(*key_backs, *out_parts)
     grad_down = product(act, joined([f.result for f in gz]))
     grad_attn = product(jnp.stack([attn_in, joined(mixed)]), jnp.stack([gq, joined(gys)]))
     grad_down, grad_attn, up_part = line.settle(grad_down, grad_attn, up_part)
@@ -870,9 +870,9 @@
     line.launch(*key_backs, grad_attn, up_line)
     line.settle()
     line.finish(up_line)
-    up_all = lax.all_gather(up_line.result, "ctx", axis=0, tiled=True)
-    line.launch(*key_backs, grad_attn)
-    line.settle()
+    line.launch(*key_backs, grad_attn, *out_parts)
+    up_row = line.settle(up_line.result)
+    up_all = lax.all_gather(up_row, "ctx", axis=0, tiled=True)
     line.finish(*key_backs)
     line.launch(grad_attn)
     gkv = unturn(joined([f.result for f in key_backs]), cosine, sine)

time: 1530 us -> 1530 us (level)
    ppermute x4, waiting for transfers between devices: 164 us -> 82.4 us  [move(): return lambda value: lax.ppermute(value, 'ctx', pairs)]
    all_gather x1, waiting for transfers between devices: 0.01 us -> 44.3 us  [local(): down_all = lax.all_gather(down_part, 'ctx', axis=0, tiled=True)]
    ppermute x66, waiting for transfers between devices: 159 us -> 201 us  [fswap(): lax.ppermute(value, 'fsdp', [(i, i ^ bits) for i in range(plane())])]
    unnamed x347 -> x351, local copies, waits for them, and re-layouts: 100 us -> 103 us
  transfers between devices with their start and end apart: 110 -> 110, of which waited for: 33 -> 34; matrix products, arithmetic and copies ran while one was open for 28% -> 29% of each run, Pallas kernels for 19% -> 19%
where the time goes in v3:
time: 1530 us; the launch traced here: 1520 us
  waiting for transfers between devices  518 us (34%)
  local copies, waits for them, and re-layouts  312 us (20%)
  Pallas kernels  288 us (19%)
  other arithmetic  197 us (13%)
  starting transfers between devices  138 us (9%)
  matrix products  47.1 us (3%)
  between operations  16.7 us (1%)
    ppermute x66, waiting for transfers between devices, fswap(): lax.ppermute(value, 'fsdp', [(i, i ^ bits) for i in range(plane())])  201 us
    ppermute x34, waiting for transfers between devices, cswap(): lax.ppermute(value, 'ctx', [(i, i ^ bits) for i in range(lax.axis_size('c...  156 us
    pallas_call x2, Pallas kernels, feed_forward(): pl.pallas_call(kernel, out_shape=(wide, jax.ShapeDtypeStruct((2,) + wide....  135 us
    unnamed x351, local copies, waits for them, and re-layouts  103 us
    pallas_call x4, Pallas kernels, product(): pl.pallas_call(product_kernel, out_shape=jax.ShapeDtypeStruct((count, sta...  86.9 us
    ppermute x4, waiting for transfers between devices, move(): return lambda value: lax.ppermute(value, 'ctx', pairs)  82.4 us
    dynamic_update_slice x42, local copies, waits for them, and re-layouts, put_rows(): return lax.dynamic_update_slice_in_dim(target, value, start, axis=0)  78.6 us
    ppermute x66, starting transfers between devices, fswap(): lax.ppermute(value, 'fsdp', [(i, i ^ bits) for i in range(plane())])  75.2 us
  transfers between devices with their start and end apart: 110, of which 34 were waited for; matrix products, arithmetic and copies ran while one was open for 29% of the time, Pallas kernels for 19%

profile of v3, /device:TPU:0, one launch (start us, length us, event | category | flops | bytes accessed | tf_op | source)
XLA Modules:
  0.0 1516.2 jit_solution(9541376515748849363)
XLA Ops:
  53.6 16.4 %collective-permute-done.5.refs_3_ = bf16[256,2048]{1,0:T(8,128)(2,1)} collective-permute-done((bf16[256,2048]{1,0:T(8,128)(2,1)}, bf16[256,2048]{1,0:T(8,128)(2,1)}, u32[]{:S(2)}, u32[]{:S(2)}) %collective-permute-start.5) | collective-permute-done | bytes 1048608 | tf_op jit(solution)/shard_map/ppermute | solution.py:404
  103.6 8.8 shard_map.207.refs_6_
  173.4 13.8 collective-permute-done.23.refs_4_
  217.1 8.8 shard_map.211.q_ref
  261.0 24.2 %all-gather.7.cloned.1.call-done.kv_ref = bf16[2048,2048]{1,0:T(8,128)(2,1)} async-done(((bf16[256,2048]{1,0:T(8,128)(2,1)}), bf16[2048,2048]{1,0:T(8,128)(2,1)}) %all-gather.7.cloned.1.call-update) | async-done | bytes 8388624 | tf_op jit(solution)/shard_map/all_gather | solution.py:765
  413.8 16.6 %collective-permute-done.50.refs_1_ = bf16[256,2048]{1,0:T(8,128)(2,1)} collective-permute-done((bf16[256,2048]{1,0:T(8,128)(2,1)S(1)}, bf16[256,2048]{1,0:T(8,128)(2,1)}, u32[]{:S(2)}, u32[]{:S(2)}) %collective-permute-start.50) | collective-permute-done | bytes 1048608 | tf_op jit(solution)/shard_map/ppermute | solution.py:404
  450.5 67.9 %shard_map.220 = (bf16[2048,2048]{1,0:T(8,128)(2,1)}, bf16[2,2048,2048]{2,1,0:T(8,128)(2,1)}, bf16[1024,2048]{1,0:T(8,128)(2,1)}, bf16[1024,2048]{1,0:T(8,128)(2,1)}) custom-call(bf16[1024,2048]{1,0:T(8,128)(2,1)} %get-tuple-element.475.refs_0_, bf16[1,1024,2048]{2,1,0:T(8,128)(2,1)} %bitcast.168, ...), custom_call_target="tpu_custom_call" | custom-call | tf_op jit(solution)/shard_map/pallas_call | solution.py:375
  540.1 67.5 %shard_map.223 = (bf16[2048,2048]{1,0:T(8,128)(2,1)}, bf16[2,2048,2048]{2,1,0:T(8,128)(2,1)}, bf16[1024,2048]{1,0:T(8,128)(2,1)}, bf16[1024,2048]{1,0:T(8,128)(2,1)}) custom-call(bf16[1024,2048]{1,0:T(8,128)(2,1)} %get-tuple-element.471.refs_0_, bf16[1,1024,2048]{2,1,0:T(8,128)(2,1)} %bitcast.167, ...), custom_call_target="tpu_custom_call", output_to_operand_aliasing={{0}: (5, {}), {1}: (6, {})} | custom-call | tf_op jit(solution)/shard_map/pallas_call | solution.py:375
  618.7 41.3 %shard_map.226.refs_4_ = bf16[2048,4096]{1,0:T(8,128)(2,1)} custom-call(bf16[1,2048,2048]{2,1,0:T(8,128)(2,1)} %bitcast.26.left_ref, bf16[2,2048,2048]{2,1,0:T(8,128)(2,1)} %get-tuple-element.274.right_ref), custom_call_target="tpu_custom_call" | custom-call | tf_op jit(solution)/shard_map/pallas_call | solution.py:86
  695.1 11.4 shard_map.228
  706.6 9.3 convolution_convert_fusion.refs_3_
  724.6 11.8 shard_map.232
  751.8 28.3 %collective-permute-start.64 = (bf16[256,2048]{1,0:T(8,128)(2,1)}, bf16[256,2048]{1,0:T(8,128)(2,1)S(1)}, u32[]{:S(2)}, u32[]{:S(2)}) collective-permute-start(bf16[256,2048]{1,0:T(8,128)(2,1)} %get-tuple-element.296), channel_id=1, source_target_pairs={{0,8},{4,12},{8,0},{12,4},{16,24},{20,28},{24,16},{28,20},{1,9},{5... | collective-permute-start | bytes 3145736 | tf_op jit(solution)/shard_map/ppermute | solution.py:408
  783.4 23.3 %shard_map.235.refs_6_ = bf16[2048,2048]{1,0:T(8,128)(2,1)} custom-call(bf16[1,2048,2048]{2,1,0:T(8,128)(2,1)} %bitcast.162, bf16[1,2048,2048]{2,1,0:T(8,128)(2,1)} %bitcast.166), custom_call_target="tpu_custom_call" | custom-call | tf_op jit(solution)/shard_map/pallas_call | solution.py:86
  811.2 21.5 %collective-permute-done.64.refs_0_ = bf16[256,2048]{1,0:T(8,128)(2,1)S(1)} collective-permute-done((bf16[256,2048]{1,0:T(8,128)(2,1)}, bf16[256,2048]{1,0:T(8,128)(2,1)S(1)}, u32[]{:S(2)}, u32[]{:S(2)}) %collective-permute-start.64) | collective-permute-done | bytes 1048608 | tf_op jit(solution)/shard_map/ppermute | solution.py:408
  837.0 15.4 %shard_map.236.refs_7_ = bf16[2048,4096]{1,0:T(8,128)(2,1)} custom-call(bf16[2,512,2048]{2,1,0:T(8,128)(2,1)S(1)} %pad_maximum_fusion.left_ref, bf16[2,512,2048]{2,1,0:T(8,128)(2,1)} %pad_maximum_fusion.1.right_ref), custom_call_target="tpu_custom_call" | custom-call | tf_op jit(solution)/shard_map/pallas_call | solution.py:86
  858.0 8.6 reduce-scatter.3.cloned.1.call-done.refs_8_
  928.2 59.1 %collective-permute-done.70.refs_0_ = bf16[256,2048]{1,0:T(8,128)(2,1)} collective-permute-done((bf16[256,2048]{1,0:T(8,128)(2,1)}, bf16[256,2048]{1,0:T(8,128)(2,1)}, u32[]{:S(2)}, u32[]{:S(2)}) %collective-permute-start.70) | collective-permute-done | bytes 1048608 | tf_op jit(solution)/shard_map/ppermute | solution.py:413
  1016.5 48.8 %collective-permute-done.81.refs_4_ = bf16[128,2048]{1,0:T(8,128)(2,1)} collective-permute-done((bf16[128,2048]{1,0:T(8,128)(2,1)}, bf16[128,2048]{1,0:T(8,128)(2,1)}, u32[]{:S(2)}, u32[]{:S(2)}) %collective-permute-start.81) | collective-permute-done | bytes 524320 | tf_op jit(solution)/shard_map/ppermute | solution.py:404
  1078.9 9.2 collective-permute-done.84.refs_7_
  1088.1 23.3 %collective-permute-done.77.refs_0_ = bf16[256,2048]{1,0:T(8,128)(2,1)} collective-permute-done((bf16[256,2048]{1,0:T(8,128)(2,1)}, bf16[256,2048]{1,0:T(8,128)(2,1)}, u32[]{:S(2)}, u32[]{:S(2)}) %collective-permute-start.77) | collective-permute-done | bytes 1048608 | tf_op jit(solution)/shard_map/ppermute | solution.py:413
  1130.3 10.2 shard_map.244.refs_3_
  1154.3 9.6 fusion.35
  1164.0 8.5 multiply_reduce_fusion
  1186.1 22.1 %collective-permute-done.88.refs_0_ = bf16[256,2048]{1,0:T(8,128)(2,1)S(1)} collective-permute-done((bf16[256,2048]{1,0:T(8,128)(2,1)}, bf16[256,2048]{1,0:T(8,128)(2,1)S(1)}, u32[]{:S(2)}, u32[]{:S(2)}) %collective-permute-start.88) | collective-permute-done | bytes 1048608 | tf_op jit(solution)/shard_map/ppermute | solution.py:404
  1224.0 8.5 collective-permute-done.91.refs_0_
  1236.1 9.8 maximum_maximum_fusion
  1255.3 115.8 %collective-permute-done.97.refs_3_ = f32[2,2048]{1,0:T(2,128)S(1)} collective-permute-done((f32[2,2048]{1,0:T(2,128)S(1)}, f32[2,2048]{1,0:T(2,128)S(1)}, u32[]{:S(2)}, u32[]{:S(2)}) %collective-permute-start.97) | collective-permute-done | bytes 16416 | tf_op jit(solution)/shard_map/ppermute | solution.py:408
  1381.9 16.9 %slice_convert_fusion = (f32[512,8192]{1,0:T(8,128)}, f32[512,8192]{1,0:T(8,128)}) fusion(bf16[512,16384]{1,0:T(8,128)(2,1)} %get-tuple-element.369), kind=kLoop, calls=%fused_computation.1 | loop fusion | flops 8388608 | bytes 50331648 | tf_op jit(solution)/shard_map/convert_element_type | solution.py:899
  1398.8 44.3 %all-gather.11.cloned.1.call-done.refs_6_ = bf16[2048,2048]{1,0:T(8,128)(2,1)} async-done(((bf16[256,2048]{1,0:T(8,128)(2,1)}), bf16[2048,2048]{1,0:T(8,128)(2,1)}) %all-gather.11.cloned.1.call-update) | async-done | bytes 8388624 | tf_op jit(solution)/shard_map/all_gather | solution.py:890
  1443.1 17.7 %collective-permute-done.99.refs_1_ = bf16[64,6144]{1,0:T(8,128)(2,1)} collective-permute-done((bf16[64,6144]{1,0:T(8,128)(2,1)}, bf16[64,6144]{1,0:T(8,128)(2,1)}, u32[]{:S(2)}, u32[]{:S(2)}) %collective-permute-start.99) | collective-permute-done | bytes 786464 | tf_op jit(solution)/shard_map/ppermute | solution.py:408
  1479.6 11.7 convert_element_type.452.refs_2_
  (841 shorter events, 689.1 us)
Async XLA Ops:
  7.2 224.3 %all-gather.5.cloned.1.call-start = ((), (), s32[]{:S(2)}) async-start(), calls=%async_computation.2 | async-start | bytes 9437184 | tf_op jit(solution)/shard_map/all_gather | solution.py:765
  119.8 165.3 %all-gather.7.cloned.1.call-start = ((), (), s32[]{:S(2)}) async-start(), calls=%async_computation.3 | async-start | bytes 9437184 | tf_op jit(solution)/shard_map/all_gather | solution.py:765
  120.6 746.0 %reduce-scatter.3.cloned.1.call-start = ((), (), s32[]{:S(2)}) async-start(), calls=%async_computation.4 | async-start | bytes 18874368 | tf_op jit(solution)/shard_map/reduce_scatter | solution.py:831
  172.1 73.1 %collective-permute-start.31 = (bf16[256,2048]{1,0:T(8,128)(2,1)}, bf16[256,2048]{1,0:T(8,128)(2,1)}, u32[]{:S(2)}, u32[]{:S(2)}) collective-permute-start(bf16[256,2048]{1,0:T(8,128)(2,1)} %get-tuple-element.414), channel_id=1, source_target_pairs={{0,1},{1,0},{2,3},{3,2},{4,5},{5,4},{6,7},{7,6},{8,9},{9,8},{10,11... | collective-permute-start | bytes 3145736 | tf_op jit(solution)/shard_map/ppermute | solution.py:404
  190.0 60.2 %collective-permute-start.30 = (bf16[256,2048]{1,0:T(8,128)(2,1)}, bf16[256,2048]{1,0:T(8,128)(2,1)}, u32[]{:S(2)}, u32[]{:S(2)}) collective-permute-start(bf16[256,2048]{1,0:T(8,128)(2,1)} %get-tuple-element.212), channel_id=1, source_target_pairs={{0,4},{4,0},{8,12},{12,8},{16,20},{20,16},{24,28},{28,24},{1,5},{5... | collective-permute-start | bytes 3145736 | tf_op jit(solution)/shard_map/ppermute | solution.py:408
  248.6 66.4 %collective-permute-start.40 = (bf16[256,2048]{1,0:T(8,128)(2,1)}, bf16[256,2048]{1,0:T(8,128)(2,1)}, u32[]{:S(2)}, u32[]{:S(2)}) collective-permute-start(bf16[256,2048]{1,0:T(8,128)(2,1)} %pad_maximum_fusion.14), channel_id=1, source_target_pairs={{0,2},{1,3},{2,0},{3,1},{4,6},{5,7},{6,4},{7,5},{8,10},{9,11},{10,... | collective-permute-start | bytes 3145736 | tf_op jit(solution)/shard_map/ppermute | solution.py:404
  250.2 70.4 %collective-permute-start.41 = (bf16[256,2048]{1,0:T(8,128)(2,1)}, bf16[256,2048]{1,0:T(8,128)(2,1)}, u32[]{:S(2)}, u32[]{:S(2)}) collective-permute-start(bf16[256,2048]{1,0:T(8,128)(2,1)} %pad_maximum_fusion.15), channel_id=1, source_target_pairs={{0,1},{1,0},{2,3},{3,2},{4,5},{5,4},{6,7},{7,6},{8,9},{9,8},{10,11... | collective-permute-start | bytes 3145736 | tf_op jit(solution)/shard_map/ppermute | solution.py:404
  443.2 77.9 %collective-permute-start.54 = (bf16[256,2048]{1,0:T(8,128)(2,1)}, bf16[256,2048]{1,0:T(8,128)(2,1)}, u32[]{:S(2)}, u32[]{:S(2)}) collective-permute-start(bf16[256,2048]{1,0:T(8,128)(2,1)} %pad_maximum_fusion.21), channel_id=1, source_target_pairs={{0,1},{1,0},{2,3},{3,2},{4,5},{5,4},{6,7},{7,6},{8,9},{9,8},{10,11... | collective-permute-start | bytes 3145736 | tf_op jit(solution)/shard_map/ppermute | solution.py:404
  446.1 75.1 %collective-permute-start.53 = (bf16[256,2048]{1,0:T(8,128)(2,1)}, bf16[256,2048]{1,0:T(8,128)(2,1)}, u32[]{:S(2)}, u32[]{:S(2)}) collective-permute-start(bf16[256,2048]{1,0:T(8,128)(2,1)} %pad_maximum_fusion.20), channel_id=1, source_target_pairs={{0,2},{1,3},{2,0},{3,1},{4,6},{5,7},{6,4},{7,5},{8,10},{9,11},{10,... | collective-permute-start | bytes 3145736 | tf_op jit(solution)/shard_map/ppermute | solution.py:404
  528.2 79.5 %collective-permute-start.55 = (bf16[256,2048]{1,0:T(8,128)(2,1)}, bf16[256,2048]{1,0:T(8,128)(2,1)}, u32[]{:S(2)}, u32[]{:S(2)}) collective-permute-start(bf16[256,2048]{1,0:T(8,128)(2,1)} %get-tuple-element.257), channel_id=1, source_target_pairs={{0,2},{1,3},{2,0},{3,1},{4,6},{5,7},{6,4},{7,5},{8,10},{9,11},{10,... | collective-permute-start | bytes 3145736 | tf_op jit(solution)/shard_map/ppermute | solution.py:404
  529.7 77.9 %collective-permute-start.56 = (bf16[256,2048]{1,0:T(8,128)(2,1)}, bf16[256,2048]{1,0:T(8,128)(2,1)}, u32[]{:S(2)}, u32[]{:S(2)}) collective-permute-start(bf16[256,2048]{1,0:T(8,128)(2,1)} %get-tuple-element.258), channel_id=1, source_target_pairs={{0,1},{1,0},{2,3},{3,2},{4,5},{5,4},{6,7},{7,6},{8,9},{9,8},{10,11... | collective-permute-start | bytes 3145736 | tf_op jit(solution)/shard_map/ppermute | solution.py:404
  660.7 488.4 %reduce-scatter.5.cloned.1.call-start = ((), (), s32[]{:S(2)}) async-start(), calls=%async_computation.5 | async-start | bytes 9437184 | tf_op jit(solution)/shard_map/reduce_scatter | solution.py:867
  746.6 111.4 %collective-permute-start.65 = (bf16[512,2048]{1,0:T(8,128)(2,1)}, bf16[512,2048]{1,0:T(8,128)(2,1)}, u32[]{:S(2)}, u32[]{:S(2)}) collective-permute-start(bf16[512,2048]{1,0:T(8,128)(2,1)} %get-tuple-element.297), channel_id=1, source_target_pairs={{0,4},{4,0},{8,12},{12,8},{16,20},{20,16},{24,28},{28,24},{1,5},{5... | collective-permute-start | bytes 6291464 | tf_op jit(solution)/shard_map/ppermute | solution.py:408
  751.8 80.8 %collective-permute-start.64 = (bf16[256,2048]{1,0:T(8,128)(2,1)}, bf16[256,2048]{1,0:T(8,128)(2,1)S(1)}, u32[]{:S(2)}, u32[]{:S(2)}) collective-permute-start(bf16[256,2048]{1,0:T(8,128)(2,1)} %get-tuple-element.296), channel_id=1, source_target_pairs={{0,8},{4,12},{8,0},{12,4},{16,24},{20,28},{24,16},{28,20},{1,9},{5... | collective-permute-start | bytes 3145736 | tf_op jit(solution)/shard_map/ppermute | solution.py:408
  872.0 499.2 %all-gather.9.cloned.1.call-start = ((), (), s32[]{:S(2)}) async-start(), calls=%async_computation.6 | async-start | bytes 18874368 | tf_op jit(solution)/shard_map/all_gather | solution.py:875
  883.0 104.3 %collective-permute-start.73 = (bf16[4,256,4096]{2,1,0:T(8,128)(2,1)}, bf16[4,256,4096]{2,1,0:T(8,128)(2,1)}, u32[]{:S(2)}, u32[]{:S(2)}) collective-permute-start(bf16[4,256,4096]{2,1,0:T(8,128)(2,1)} %get-tuple-element.314), channel_id=1, source_target_pairs={{0,4},{4,0},{8,12},{12,8},{16,20},{20,16},{24,28},{28,24},{1,5},{5... | collective-permute-start | bytes 25165832 | tf_op jit(solution)/shard_map/ppermute | solution.py:408
  889.8 97.5 %collective-permute-start.70 = (bf16[256,2048]{1,0:T(8,128)(2,1)}, bf16[256,2048]{1,0:T(8,128)(2,1)}, u32[]{:S(2)}, u32[]{:S(2)}) collective-permute-start(bf16[256,2048]{1,0:T(8,128)(2,1)} %get-tuple-element.311), channel_id=1, source_target_pairs={{16,0},{20,4},{24,8},{28,12},{17,1},{21,5},{25,9},{29,13},{18,2},{... | collective-permute-start | bytes 3145736 | tf_op jit(solution)/shard_map/ppermute | solution.py:413
  891.0 96.2 %collective-permute-start.71 = (bf16[256,2048]{1,0:T(8,128)(2,1)}, bf16[256,2048]{1,0:T(8,128)(2,1)}, u32[]{:S(2)}, u32[]{:S(2)}) collective-permute-start(bf16[256,2048]{1,0:T(8,128)(2,1)} %get-tuple-element.312), channel_id=1, source_target_pairs={{20,16},{24,20},{28,24},{21,17},{25,21},{29,25},{22,18},{26,22},{3... | collective-permute-start | bytes 3145736 | tf_op jit(solution)/shard_map/ppermute | solution.py:413
  892.7 94.5 %collective-permute-start.72 = (bf16[256,2048]{1,0:T(8,128)(2,1)}, bf16[256,2048]{1,0:T(8,128)(2,1)}, u32[]{:S(2)}, u32[]{:S(2)}) collective-permute-start(bf16[256,2048]{1,0:T(8,128)(2,1)} %get-tuple-element.313), channel_id=1, source_target_pairs={{0,8},{4,12},{8,0},{12,4},{16,24},{20,28},{24,16},{28,20},{1,9},{5... | collective-permute-start | bytes 3145736 | tf_op jit(solution)/shard_map/ppermute | solution.py:408
  1003.6 107.8 %collective-permute-start.79 = (bf16[256,4096]{1,0:T(8,128)(2,1)}, bf16[256,4096]{1,0:T(8,128)(2,1)}, u32[]{:S(2)}, u32[]{:S(2)}) collective-permute-start(bf16[256,4096]{1,0:T(8,128)(2,1)} %get-tuple-element.324), channel_id=1, source_target_pairs={{0,2},{1,3},{2,0},{3,1},{4,6},{5,7},{6,4},{7,5},{8,10},{9,11},{10,... | collective-permute-start | bytes 6291464 | tf_op jit(solution)/shard_map/ppermute | solution.py:404
  1005.2 106.1 %collective-permute-start.80 = (bf16[256,4096]{1,0:T(8,128)(2,1)}, bf16[256,4096]{1,0:T(8,128)(2,1)}, u32[]{:S(2)}, u32[]{:S(2)}) collective-permute-start(bf16[256,4096]{1,0:T(8,128)(2,1)} %get-tuple-element.325), channel_id=1, source_target_pairs={{0,1},{1,0},{2,3},{3,2},{4,5},{5,4},{6,7},{7,6},{8,9},{9,8},{10,11... | collective-permute-start | bytes 6291464 | tf_op jit(solution)/shard_map/ppermute | solution.py:404
  1005.7 59.6 %collective-permute-start.81 = (bf16[128,2048]{1,0:T(8,128)(2,1)}, bf16[128,2048]{1,0:T(8,128)(2,1)}, u32[]{:S(2)}, u32[]{:S(2)}) collective-permute-start(bf16[128,2048]{1,0:T(8,128)(2,1)} %get-tuple-element.326), channel_id=1, source_target_pairs={{0,1},{1,0},{2,3},{3,2},{4,5},{5,4},{6,7},{7,6},{8,9},{9,8},{10,11... | collective-permute-start | bytes 1572872 | tf_op jit(solution)/shard_map/ppermute | solution.py:404
  1007.6 67.6 %collective-permute-start.83 = (bf16[128,2048]{1,0:T(8,128)(2,1)}, bf16[128,2048]{1,0:T(8,128)(2,1)}, u32[]{:S(2)}, u32[]{:S(2)}) collective-permute-start(bf16[128,2048]{1,0:T(8,128)(2,1)} %get-tuple-element.328), channel_id=1, source_target_pairs={{0,1},{1,0},{2,3},{3,2},{4,5},{5,4},{6,7},{7,6},{8,9},{9,8},{10,11... | collective-permute-start | bytes 1572872 | tf_op jit(solution)/shard_map/ppermute | solution.py:404
  1111.4 331.6 %all-gather.11.cloned.1.call-start = ((), (), s32[]{:S(2)}) async-start(), calls=%async_computation.7 | async-start | bytes 9437184 | tf_op jit(solution)/shard_map/all_gather | solution.py:890
  1246.2 124.9 %collective-permute-start.94 = (bf16[64,6144]{1,0:T(8,128)(2,1)S(1)}, bf16[64,6144]{1,0:T(8,128)(2,1)S(1)}, u32[]{:S(2)}, u32[]{:S(2)}) collective-permute-start(bf16[64,6144]{1,0:T(8,128)(2,1)S(1)} %get-tuple-element.441), channel_id=1, source_target_pairs={{0,8},{4,12},{8,0},{12,4},{16,24},{20,28},{24,16},{28,20},{1,9},{5... | collective-permute-start | bytes 2359304 | tf_op jit(solution)/shard_map/ppermute | solution.py:408
  1248.0 123.1 %collective-permute-start.95 = (bf16[64,6144]{1,0:T(8,128)(2,1)S(1)}, bf16[64,6144]{1,0:T(8,128)(2,1)}, u32[]{:S(2)}, u32[]{:S(2)}) collective-permute-start(bf16[64,6144]{1,0:T(8,128)(2,1)S(1)} %get-tuple-element.440), channel_id=1, source_target_pairs={{0,16},{4,20},{8,24},{12,28},{16,0},{20,4},{24,8},{28,12},{1,17},{... | collective-permute-start | bytes 2359304 | tf_op jit(solution)/shard_map/ppermute | solution.py:408
  1248.0 123.2 %collective-permute-start.96 = (bf16[64,6144]{1,0:T(8,128)(2,1)S(1)}, bf16[64,6144]{1,0:T(8,128)(2,1)}, u32[]{:S(2)}, u32[]{:S(2)}) collective-permute-start(bf16[64,6144]{1,0:T(8,128)(2,1)S(1)} %get-tuple-element.439), channel_id=1, source_target_pairs={{0,24},{4,28},{8,16},{12,20},{16,8},{20,12},{24,0},{28,4},{1,25},{... | collective-permute-start | bytes 2359304 | tf_op jit(solution)/shard_map/ppermute | solution.py:408
  1252.8 118.3 %collective-permute-start.97 = (f32[2,2048]{1,0:T(2,128)S(1)}, f32[2,2048]{1,0:T(2,128)S(1)}, u32[]{:S(2)}, u32[]{:S(2)}) collective-permute-start(f32[2,2048]{1,0:T(2,128)S(1)} %add.752), channel_id=1, source_target_pairs={{0,16},{4,20},{8,24},{12,28},{16,0},{20,4},{24,8},{28,12},{1,17},{... | collective-permute-start | bytes 49160 | tf_op jit(solution)/shard_map/ppermute | solution.py:408
  1375.2 67.9 %collective-permute-start.100 = (bf16[64,6144]{1,0:T(8,128)(2,1)}, bf16[64,6144]{1,0:T(8,128)(2,1)}, u32[]{:S(2)}, u32[]{:S(2)}) collective-permute-start(bf16[64,6144]{1,0:T(8,128)(2,1)} %add_convert_fusion.6), channel_id=1, source_target_pairs={{0,24},{4,28},{8,16},{12,20},{16,8},{20,12},{24,0},{28,4},{1,25},{... | collective-permute-start | bytes 2359304 | tf_op jit(solution)/shard_map/ppermute | solution.py:408
  1375.2 67.9 %collective-permute-start.98 = (bf16[64,6144]{1,0:T(8,128)(2,1)}, bf16[64,6144]{1,0:T(8,128)(2,1)S(1)}, u32[]{:S(2)}, u32[]{:S(2)}) collective-permute-start(bf16[64,6144]{1,0:T(8,128)(2,1)} %add_convert_fusion.6), channel_id=1, source_target_pairs={{0,8},{4,12},{8,0},{12,4},{16,24},{20,28},{24,16},{28,20},{1,9},{5... | collective-permute-start | bytes 2359304 | tf_op jit(solution)/shard_map/ppermute | solution.py:408
  1375.2 85.5 %collective-permute-start.99 = (bf16[64,6144]{1,0:T(8,128)(2,1)}, bf16[64,6144]{1,0:T(8,128)(2,1)}, u32[]{:S(2)}, u32[]{:S(2)}) collective-permute-start(bf16[64,6144]{1,0:T(8,128)(2,1)} %add_convert_fusion.6), channel_id=1, source_target_pairs={{0,16},{4,20},{8,24},{12,28},{16,0},{20,4},{24,8},{28,12},{1,17},{... | collective-permute-start | bytes 2359304 | tf_op jit(solution)/shard_map/ppermute | solution.py:408
  1380.3 62.8 %collective-permute-start.101 = (f32[2,2048]{1,0:T(2,128)S(1)}, f32[2,2048]{1,0:T(2,128)S(1)}, u32[]{:S(2)}, u32[]{:S(2)}) collective-permute-start(f32[2,2048]{1,0:T(2,128)S(1)} %add.756), channel_id=1, source_target_pairs={{0,1},{1,0},{2,3},{3,2},{4,5},{5,4},{6,7},{7,6},{8,9},{9,8},{10,11... | collective-permute-start | bytes 49160 | tf_op jit(solution)/shard_map/ppermute | solution.py:404
  (235 other events, 5032.9 us)
Sparse Core Ops, SparseCore 0:
  120.0 82.3 all-gather.4
  204.6 80.5 all-gather.6
  660.9 205.6 reduce-scatter.2
  872.1 164.0 reduce-scatter.4
  1111.5 166.1 all-gather.8
  1279.2 163.7 all-gather.10
